TPU v7x, 32 devices: a whole 2x2x4 slice. The times are simulated.
32 devices in a mesh: dp: 8 (over z, x), head: 4 (over y, core).
Axes of the slice: x: 2, y: 2, z: 4, core: 2. Of those that a mesh axis runs over, the one named last changes fastest.
Arguments:
- layer_input: bfloat16 [512, 32, 768], P('head', 'dp'), may hold values from -6 to 6
- lengths: int32 [32], P('dp'), may hold values from 64 to 512, as said below
- cotangent: bfloat16 [512, 32, 768], P('head', 'dp'), may hold values from -6 to 6
- w_qkv: float32 [3, 768, 768], P(None, 'dp', 'head'), may hold values from -0.21875 to 0.21875
- w_out: float32 [768, 768], P('head', 'dp'), may hold values from -1.75 to 1.75
- w_up: float32 [768, 3072], P(None, ('dp', 'head')), may hold values from -0.21875 to 0.21875
- w_down: float32 [3072, 768], P(('dp', 'head')), may hold values from -0.109375 to 0.109375
- vectors: float32 [9216], P(('dp', 'head')), may hold values from -0.6 to 1.45
- mom_qkv: float32 [3, 768, 768], P(None, 'dp', 'head'), may hold values from -160 to 160
- mom_out: float32 [768, 768], P('head', 'dp'), may hold values from -80 to 80
- mom_up: float32 [768, 3072], P(None, ('dp', 'head')), may hold values from -80 to 80
- mom_down: float32 [3072, 768], P(('dp', 'head')), may hold values from -160 to 160
- mom_vec: float32 [9216], P(('dp', 'head')), may hold values from -384 to 384
- avg_qkv: float32 [3, 768, 768], P(None, 'dp', 'head'), may hold values from -0.21875 to 0.21875
- avg_out: float32 [768, 768], P('head', 'dp'), may hold values from -1.75 to 1.75
- avg_up: float32 [768, 3072], P(None, ('dp', 'head')), may hold values from -0.21875 to 0.21875
- avg_down: float32 [3072, 768], P(('dp', 'head')), may hold values from -0.109375 to 0.109375
- avg_vec: float32 [9216], P(('dp', 'head')), may hold values from -3 to 3
Outputs:
- layer_output: bfloat16 [512, 32, 768], P('head', 'dp')
- grad_input: float32 [512, 32, 768], P('head', 'dp')
- grad_qkv: float32 [3, 768, 768], P(None, 'dp', 'head')
- grad_out: float32 [768, 768], P('head', 'dp')
- grad_up: float32 [768, 3072], P(None, ('dp', 'head'))
- grad_down: float32 [3072, 768], P(('dp', 'head'))
- grad_vec: float32 [9216], P(('dp', 'head'))
- new_qkv: float32 [3, 768, 768], P(None, 'dp', 'head')
- new_out: float32 [768, 768], P('head', 'dp')
- new_up: float32 [768, 3072], P(None, ('dp', 'head'))
- new_down: float32 [3072, 768], P(('dp', 'head'))
- new_vec: float32 [9216], P(('dp', 'head'))
- new_mom_qkv: float32 [3, 768, 768], P(None, 'dp', 'head')
- new_mom_out: float32 [768, 768], P('head', 'dp')
- new_mom_up: float32 [768, 3072], P(None, ('dp', 'head'))
- new_mom_down: float32 [3072, 768], P(('dp', 'head'))
- new_mom_vec: float32 [9216], P(('dp', 'head'))
- new_avg_qkv: float32 [3, 768, 768], P(None, 'dp', 'head')
- new_avg_out: float32 [768, 768], P('head', 'dp')
- new_avg_up: float32 [768, 3072], P(None, ('dp', 'head'))
- new_avg_down: float32 [3072, 768], P(('dp', 'head'))
- new_avg_vec: float32 [9216], P(('dp', 'head'))
Inputs may be any that keep to these rules, and one draw needn't show every extreme that they name: `lengths`: in each aligned block of 2 documents at least one has length 512.
All inputs are finite; a program needn't handle non-finite values.
Results may differ from a plain program's by a relative error of at most 0.013.
The roundings to bfloat16 on the way count: a program that leaves them out, or rounds other values in their place, can miss the bound.
Values may be sent and summed in bfloat16 or wider, within the bound.
No kernel may reach another device: no remote copies, remote signals or barrier semaphores. Data moves between devices by JAX's collectives and lax.ppermute only.
A program may use at most 192 MiB of HBM per device.

v0:
```python
import functools
import math

import jax
import jax.numpy as jnp
from jax import lax
from jax.experimental import pallas as pl
from jax.experimental.pallas import tpu as pltpu
from jax.sharding import Mesh
from jax.sharding import PartitionSpec as P

D = 768
HD = 64
FF = 3072
LEN = 512

EPSILON = 1e-05
MOMENTUM = 0.9
AVERAGE = 0.9
DECAY = 0.01
RATE_BASE = 0.05

BF = jnp.bfloat16
F32 = jnp.float32
NT = (((1,), (1,)), ((), ()))
NN = (((1,), (0,)), ((), ()))


def send(values, axis, bit=1):
    return lax.ppermute(values, axis, [(i, i ^ bit) for i in range(lax.axis_size(axis))])


def corner(array):
    rows, columns = min(8, array.shape[-2]), min(128, array.shape[-1])
    return array.reshape(-1, *array.shape[-2:])[0, :rows, :columns]


def after(values, *others):
    zero = sum(corner(v)[0, 0].astype(F32) * 0.0 for v in jax.tree.leaves(others))
    return jax.tree.map(lambda v: v + zero.astype(v.dtype), values)


def z_order(size):
    return jnp.array([0, 2, 1, 3]) if size == 4 else jnp.arange(size)


def flip_order(axis):
    size = lax.axis_size(axis)
    return lax.axis_index(axis) ^ z_order(size)


def gather_z(shard):
    size = lax.axis_size("z")
    if size != 4:
        whole = jnp.take(lax.all_gather(shard, "z"), flip_order("z"), axis=0)
        return whole, whole[0]
    got = send(shard, "z", 2)
    pair = jnp.stack([shard, got], 0)
    return jnp.concatenate([pair, send(pair, "z", 1)], 0), got


def total(terms):
    result = terms[0].astype(F32)
    for term in terms[1:]:
        result = result + term.astype(F32)
    return result


def swap(terms, axis, others=()):
    part = total([t[1] for t in terms])
    got = send((after(part, others) if others else part).astype(BF), axis)
    return [t[0] for t in terms] + [got]


def scatter_z(sums):
    joined = lambda index: jnp.concatenate([total([t[index] for t in terms]) for terms in sums], -2)
    if lax.axis_size("z") != 4:
        everything = jnp.take(joined(slice(None)).astype(BF), flip_order("z"), axis=0)
        parts = lax.all_to_all(everything, "z", 0, 0, tiled=True)
        return [total(list(parts[1:])), parts[0]]
    got = send(joined(slice(2, 4)).astype(BF), "z", 1)
    left, start = [], 0
    for terms in sums:
        end = start + terms[0].shape[-2]
        left.append([t[:2] for t in terms] + [got[:, start:end]])
        start = end
    sums = left
    return [joined(0), send(joined(1).astype(BF), "z", 2)]


def to_documents(values):
    y, c = lax.axis_index("y"), lax.axis_index("c")
    local, _, width = values.shape
    docs = values.transpose(1, 0, 2).reshape(2, 2, local, width)
    mine = lax.dynamic_index_in_dim(docs, y, 0, keepdims=False)
    got_y = send(lax.dynamic_index_in_dim(docs, 1 - y, 0, keepdims=False), "y")
    of = lambda v, core: lax.dynamic_index_in_dim(v, core, 0, keepdims=False)
    got = send(jnp.stack([of(mine, 1 - c), of(got_y, 1 - c)], 0), "c")
    document = jnp.stack([of(mine, c), of(got_y, c), got[0], got[1]], 0)
    return document.reshape(4 * local, width), got_y


def from_documents_y(values, local):
    values = values.reshape(2, 2, local, values.shape[1])
    return values[:, 0], send(values[:, 1], "y")


def assemble_kernel(seats_ref, own_ref, got_y_ref, got_c_ref, out_ref):
    for place, ref, part in ((0, own_ref, 0), (1, got_y_ref, 0), (2, got_c_ref, 0), (3, got_c_ref, 1)):
        out_ref[seats_ref[place]] = ref[part].astype(out_ref.dtype)


def from_documents(seats, own, got_y, dtype):
    got_c = send(jnp.stack([own[1], got_y[1]], 0), "c")
    vmem = pl.BlockSpec(memory_space=pltpu.VMEM)
    docs = pl.pallas_call(
        assemble_kernel,
        in_specs=[SMEM_SPEC, vmem, vmem, vmem],
        out_specs=vmem,
        out_shape=jax.ShapeDtypeStruct((4, *own.shape[1:]), dtype),
        compiler_params=params(12),
        cost_estimate=cost(0.0, 2.0, 0.0),
        name="assemble",
    )(seats, own, got_y, got_c)
    return docs.transpose(1, 0, 2)


def dot(a, b, dims):
    return lax.dot_general(a, b, dims, preferred_element_type=F32)


def normalized(values):
    center = values - jnp.mean(values, -1, keepdims=True)
    inverse = lax.rsqrt(jnp.mean(center * center, -1, keepdims=True) + EPSILON)
    return center * inverse, inverse


def norm_backward(d_result, normed, inverse, gain):
    d_normed = d_result * gain
    return inverse * (
        d_normed
        - jnp.mean(d_normed, -1, keepdims=True)
        - normed * jnp.mean(d_normed * normed, -1, keepdims=True)
    )


def block_start(place_ref, index, rows):
    start = place_ref[index] * rows
    return pl.multiple_of(start, 32) if rows % 32 == 0 else start


def place_weights(place_ref, qk_refs, vo_refs, w_qk, w_vo, rows):
    across, deep = len(qk_refs), qk_refs[0].shape[1]

    def place(group):
        for i in range(across):
            for k in range(deep):
                start = block_start(place_ref, i * deep + k, rows)
                w_qk[pl.ds(start, rows), :] = qk_refs[i][0, k]
                w_vo[pl.ds(start, rows), :] = vo_refs[group][i, k]

    for group in range(2):
        pl.when(pl.program_id(0) == group)(functools.partial(place, group))


def accumulate(step, target, start_ref, value):
    @pl.when(step == 0)
    def _():
        target[...] = value if start_ref is None else start_ref[...] + value

    @pl.when(step > 0)
    def _():
        target[...] += value


def attention_forward_kernel(rows, last, parts, *refs):
    qk_refs, vo_refs, refs = refs[:parts], refs[parts : parts + 2], refs[parts + 2 :]
    place_ref, x_ref, bias_ref, mask_ref, vec_ref = refs[:5]
    if last:
        mix_in, qkv_ref, lse_ref, context_ref = refs[5:9]
        h_ref, hb_ref, n_ref, inv_ref, xt_ref, w_qk, w_vo, mix_ref = refs[9:]
    else:
        mix_in = None
        qkv_ref, lse_ref, context_ref, mix_ref, w_qk, w_vo = refs[5:]
    step = pl.program_id(0)
    place_weights(place_ref, qk_refs, vo_refs, w_qk, w_vo, rows)
    x = x_ref[...]
    width = w_qk.shape[1] // 2
    bias = bias_ref[0]
    qk = dot(x, w_qk[...], NN)
    v = (dot(x, w_vo[:, :width], NN) + bias[1:2, :width]).astype(BF)
    q = ((qk[:, :width] + bias[0:1, :width]).astype(BF).astype(F32) * HD ** (-0.5)).astype(BF)
    k = qk[:, width:].astype(BF)
    qkv_ref[0, :, :width] = q
    qkv_ref[0, :, width : 2 * width] = k
    qkv_ref[0, :, 2 * width :] = v
    mask = mask_ref[0:1]
    length = x.shape[0]
    contexts, logs = [], []
    for head in range(width // HD):
        cols = slice(head * HD, (head + 1) * HD)
        s = dot(q[:, cols], k[:, cols], NT) + mask
        peak = jnp.max(s, -1, keepdims=True)
        total = jnp.sum(jnp.exp(s - peak), -1, keepdims=True)
        log_total = peak + jnp.log(total)
        p = jnp.exp(s - log_total).astype(BF)
        contexts.append(dot(p, v[:, cols], NN).astype(BF))
        logs.append(log_total)
    context = jnp.concatenate(contexts, 1)
    context_ref[0] = context
    lanes = lax.broadcasted_iota(jnp.int32, (length, 128), 1)
    packed = jnp.zeros((length, 128), F32)
    for head, log_total in enumerate(logs):
        packed = jnp.where(lanes == head, log_total, packed)
    lse_ref[0] = packed.T[:8]
    accumulate(step, mix_ref, mix_in, dot(context, w_vo[:, width:], NT))
    if last:

        @pl.when(step == pl.num_programs(0) - 1)
        def _():
            first_res = x_ref[...].astype(F32) + mix_ref[...] + vec_ref[2:3]
            normed, inverse = normalized(first_res)
            hidden = normed * vec_ref[3:4] + vec_ref[4:5]
            n_ref[...] = normed
            inv_ref[...] = jnp.broadcast_to(inverse, inv_ref.shape)
            h_ref[...] = hidden
            hb_ref[...] = hidden.astype(BF)
            xt_ref[...] = x_ref[...].T


def attention_backward_kernel(rows, last, parts, *refs):
    qk_refs, vo_refs, refs = refs[:parts], refs[parts : parts + 2], refs[parts + 2 :]
    place_ref, xt_ref, gr_ref, grt_ref, qkv_ref, lse_ref, context_ref = refs[:7]
    mask_ref, start_ref = refs[7:9]
    if last:
        gqk_ref, gvo_ref, bias_ref, out_ref, w_qk, w_vo, g_qkv, gin_ref = refs[9:]
    else:
        gqk_ref, gvo_ref, bias_ref, gin_ref, w_qk, w_vo, g_qkv = refs[9:]
    step = pl.program_id(0)
    place_weights(place_ref, qk_refs, vo_refs, w_qk, w_vo, rows)
    width = w_qk.shape[1] // 2
    gc = dot(gr_ref[...], w_vo[:, width:], NN).astype(BF)
    mask = mask_ref[:, :1]
    sums = []
    for head in range(width // HD):
        q = qkv_ref[0, :, head * HD : (head + 1) * HD]
        k = qkv_ref[0, :, width + head * HD : width + (head + 1) * HD]
        v = qkv_ref[0, :, 2 * width + head * HD : 2 * width + (head + 1) * HD]
        g = gc[:, head * HD : (head + 1) * HD]
        p = jnp.exp(dot(k, q, NT) + mask - lse_ref[0, head : head + 1])
        dp = dot(v, g, NT)
        gv = dot(p.astype(BF), g, NN)
        delta = jnp.sum(p * dp, 0, keepdims=True)
        gs = (p * (dp - delta)).astype(BF)
        gk = dot(gs, q, NN)
        gq = dot(gs.T, (k.astype(F32) * HD ** (-0.5)).astype(BF), NN)
        g_qkv[:, head * HD : (head + 1) * HD] = gq.astype(BF)
        g_qkv[:, width + head * HD : width + (head + 1) * HD] = gk.astype(BF)
        g_qkv[:, 2 * width + head * HD : 2 * width + (head + 1) * HD] = gv.astype(BF)
        sums.append((jnp.sum(gq, 0, keepdims=True), jnp.sum(gv, 0, keepdims=True)))
    bias_ref[0, 0:1, :] = jnp.concatenate([s[0] for s in sums], 1)
    bias_ref[0, 1:2, :] = jnp.concatenate([s[1] for s in sums], 1)
    g_qk = g_qkv[:, : 2 * width]
    g_v = g_qkv[:, 2 * width :]
    gin = dot(g_qk, w_qk[...], NT) + dot(g_v, w_vo[:, :width], NT)
    accumulate(step, gin_ref, start_ref, gin)

    w_qk[...] = dot(xt_ref[...], g_qk, NN).astype(BF)
    w_vo[:, :width] = dot(xt_ref[...], g_v, NN).astype(BF)
    w_vo[:, width:] = dot(grt_ref[...], context_ref[0], NN).astype(BF)
    across, deep = gqk_ref.shape[0], gqk_ref.shape[2]
    for i in range(across):
        for j in range(deep):
            start = block_start(place_ref, i * deep + j, rows)
            gqk_ref[i, 0, j] = w_qk[pl.ds(start, rows), :]
            gvo_ref[0, i, j] = w_vo[pl.ds(start, rows), :]
    if last:

        @pl.when(step == pl.num_programs(0) - 1)
        def _():
            out_ref[...] = gin_ref[...].astype(BF)


def ffn_weights(refs):
    step = pl.program_id(0)
    up = jnp.where(step < 2, refs[0][...], refs[1][...])
    down = jnp.where(step % 2 == 0, refs[2][...], refs[3][...])
    return up, down


def ffn_forward_kernel(last, *refs):
    up, down = ffn_weights(refs[:4])
    h_ref, hb_ref, bias_ref, vec_ref = refs[4:8]
    if last:
        sum_in, cot_ref, mask_ref = refs[8:11]
        act_ref, slope_ref, out_ref, gr_ref, grb_ref, vec_out, sum_ref = refs[11:]
    else:
        sum_in = None
        act_ref, slope_ref, sum_ref = refs[8:]
    step = pl.program_id(0)
    u = dot(hb_ref[...], up, NT) + bias_ref[0:1]
    phi = 0.5 + 0.5 * lax.erf(u * 0.7071067811865476)
    act = (u * phi).astype(BF)
    act_ref[...] = act
    slope_ref[...] = phi + u * jnp.exp(-0.5 * u * u) * 0.3989422804014327
    accumulate(step, sum_ref, sum_in, dot(act, down, NN))
    if last:

        @pl.when(step == pl.num_programs(0) - 1)
        def _():
            second_res = h_ref[...] + (sum_ref[...] + vec_ref[9:10])
            normed, inverse = normalized(second_res)
            out_ref[...] = (normed * vec_ref[10:11] + vec_ref[11:12]).astype(BF)
            d_result = jnp.where(mask_ref[:, :1] == 0.0, cot_ref[...].astype(F32), 0.0)
            vec_out[0:1] = jnp.sum(d_result * normed, 0, keepdims=True)
            vec_out[1:2] = jnp.sum(d_result, 0, keepdims=True)
            d_second = norm_backward(d_result, normed, inverse, vec_ref[10:11])
            vec_out[2:3] = jnp.sum(d_second, 0, keepdims=True)
            gr_ref[...] = d_second
            grb_ref[...] = d_second.astype(BF)


def ffn_backward_kernel(last, *refs):
    up, down = ffn_weights(refs[:4])
    grb_ref, hb_ref, act_ref, slope_ref, sum_in = refs[4:9]
    if last:
        n_ref, inv_ref, vec_ref = refs[9:12]
        gu_ref, gd_ref, bias_ref, gr_ref, gr1b_ref, grt_ref, vec_out, sum_ref = refs[12:]
    else:
        gu_ref, gd_ref, bias_ref, sum_ref = refs[9:]
    step = pl.program_id(0)
    grb = grb_ref[...]
    d_up = dot(grb, down, NT) * slope_ref[...]
    bias_ref[0:1] = jnp.sum(d_up, 0, keepdims=True)
    d_up_b = d_up.astype(BF)
    gd_ref[...] = dot(act_ref[...].T, grb, NN).astype(BF)
    gu_ref[...] = dot(d_up_b.T, hb_ref[...], NN).astype(BF)
    accumulate(step, sum_ref, sum_in, dot(d_up_b, up, NN))
    if last:

        @pl.when(step == pl.num_programs(0) - 1)
        def _():
            d_hidden = sum_ref[...]
            normed = n_ref[...]
            vec_out[0:1] = jnp.sum(d_hidden * normed, 0, keepdims=True)
            vec_out[1:2] = jnp.sum(d_hidden, 0, keepdims=True)
            d_first = norm_backward(d_hidden, normed, inv_ref[:, :1], vec_ref[3:4])
            vec_out[2:3] = jnp.sum(d_first, 0, keepdims=True)
            gr_ref[...] = d_first
            gr1b_ref[...] = d_first.astype(BF)
            grt_ref[...] = d_first.astype(BF).T


def whole(array):
    shape = array.shape
    return pl.BlockSpec(shape, lambda g: (0,) * len(shape))


def per_group(array):
    rest = array.shape[1:]
    return pl.BlockSpec((1, *rest), lambda g: (g, *(0 for _ in rest)))


def per_corner(array, rows, dim):
    block = [*array.shape[:3], rows, array.shape[4]]
    block[dim] = 1
    return pl.BlockSpec(tuple(block), lambda g: (0, g, 0, 0, 0) if dim else (g, 0, 0, 0, 0))


def per_rows(array, size, crossed):
    if crossed:
        return pl.BlockSpec((size, array.shape[1]), lambda g: (g % 2 * 2 + g // 2, 0))
    return pl.BlockSpec((size, array.shape[1]), lambda g: (g, 0))


def per_columns(array, size):
    return pl.BlockSpec((array.shape[0], size), lambda g: (0, g))


def spread_vectors_kernel(owner_ref, heads_ref, pieces_ref, rows_ref, up_ref, bias_ref, units):
    _, across, _, deep = COUNTS
    unit = units.shape[1]
    for x in range(2):
        for y in range(2):
            for z in range(deep):
                for c in range(2):
                    index = ((c * across + x) * 2 + y) * deep + z
                    start = owner_ref[index] * 3
                    for i in range(3):
                        units[pl.ds(start + i, 1), :] = pieces_ref[
                            x, y, z, c : c + 1, i * unit : (i + 1) * unit
                        ]
    per_row = D // unit
    for row in range(12):
        for i in range(per_row):
            rows_ref[row : row + 1, i * unit : (i + 1) * unit] = units[
                row * per_row + i : row * per_row + i + 1, :
            ]
    half = FF // 2
    for index in range(FF // unit):
        start = index * unit
        up_ref[start // half, 0:1, start % half : start % half + unit] = units[
            pl.ds(5 * per_row + owner_ref[index], 1), :
        ]
    width = bias_ref.shape[2]
    for group in range(4):
        for kind in range(2):
            for i in range(width // unit):
                start = kind * per_row + heads_ref[group] * (width // unit) + i
                bias_ref[group, kind : kind + 1, i * unit : (i + 1) * unit] = units[
                    pl.ds(start, 1), :
                ]


def collect_vectors_kernel(
    owner_ref, heads_ref, bias_0, bias_1, up_0, up_1, one_ref, two_ref, out_ref, units
):
    out_ref[...] = jnp.zeros(out_ref.shape, F32)
    unit = units.shape[1]
    per_row = D // unit
    width = bias_0.shape[2]
    for group in range(4):
        source = (bias_0, bias_1)[group // 2]
        for kind in range(2):
            for i in range(width // unit):
                start = kind * per_row + heads_ref[group] * (width // unit) + i
                units[pl.ds(start, 1), :] = source[
                    group % 2, kind : kind + 1, i * unit : (i + 1) * unit
                ]
    half = FF // 2
    for index in range(FF // unit):
        source = (up_0, up_1)[index * unit // half]
        start = index * unit % half
        units[pl.ds(5 * per_row + owner_ref[index], 1), :] = source[0:1, start : start + unit]
    for row, source, line in (
        (2, one_ref, 2),
        (3, one_ref, 0),
        (4, one_ref, 1),
        (9, two_ref, 2),
        (10, two_ref, 0),
        (11, two_ref, 1),
    ):
        for i in range(per_row):
            units[row * per_row + i : row * per_row + i + 1, :] = source[
                line : line + 1, i * unit : (i + 1) * unit
            ]
    for index in range(FF // unit):
        for i in range(3):
            out_ref[index, 0:1, i * unit : (i + 1) * unit] = units[
                pl.ds(owner_ref[index] * 3 + i, 1), :
            ]


COUNTS = (2, 2, 2, 4)


def spread_vectors(owner, heads, pieces, unit, width):
    outs = [like((12, D), F32), like((2, 8, FF // 2), F32), like((4, 8, width), F32)]
    return pl.pallas_call(
        spread_vectors_kernel,
        in_specs=[SMEM_SPEC, SMEM_SPEC, pl.BlockSpec(memory_space=pltpu.VMEM)],
        out_specs=[pl.BlockSpec(memory_space=pltpu.VMEM)] * 3,
        out_shape=outs,
        scratch_shapes=[pltpu.VMEM((12 * D // unit, unit), F32)],
        compiler_params=params(8),
        cost_estimate=cost(0.0, 0.5, 0.0),
        name="spread_vectors",
    )(owner, heads, pieces)


def collect_vectors(owner, heads, unit, pair, *sources):
    return pl.pallas_call(
        collect_vectors_kernel,
        in_specs=[SMEM_SPEC, SMEM_SPEC] + [pl.BlockSpec(memory_space=pltpu.VMEM)] * len(sources),
        out_specs=pl.BlockSpec(memory_space=pltpu.VMEM),
        out_shape=like((FF // unit, 8, pair), F32),
        scratch_shapes=[pltpu.VMEM((12 * D // unit, unit), F32)],
        compiler_params=params(8),
        cost_estimate=cost(0.0, 0.5, 0.0),
        name="collect_vectors",
    )(owner, heads, *sources)


def advance_attention_kernel(rates, *refs):
    terms, olds, outs = refs[:2], refs[2:8], refs[8:]
    whole_sum = terms[0][...]
    for term in terms[1:]:
        whole_sum = whole_sum + term[...].astype(F32)
    rows, width = olds[0].shape[1], olds[0].shape[2]
    parts = [
        whole_sum[:rows, :width],
        whole_sum[:rows, width:],
        whole_sum[rows + 8 :, :width],
    ]
    for i, grad in enumerate(parts):
        new = advance(olds[0][i], grad, olds[1][i], olds[2][i], DECAY, rates[0])
        for ref, value in zip(outs[:4], (grad, *new)):
            ref[i] = value
    grad = whole_sum[rows + 8 :, width:].T
    new = advance(olds[3][...], grad, olds[4][...], olds[5][...], DECAY, rates[1])
    for ref, value in zip(outs[4:8], (grad, *new)):
        ref[...] = value
    outs[8][...] = whole_sum[rows : rows + 8]


def advance_attention(terms, qkv, out, rates):
    outs = [like(qkv[0].shape, F32)] * 4 + [like(out[0].shape, F32)] * 4
    outs.append(like((8, terms[0].shape[1]), F32))
    vmem = pl.BlockSpec(memory_space=pltpu.VMEM)
    return pl.pallas_call(
        functools.partial(advance_attention_kernel, rates),
        in_specs=[vmem] * 8,
        out_specs=[vmem] * 9,
        out_shape=outs,
        compiler_params=params(16),
        cost_estimate=cost(0.0, 3.0, 0.0),
        name="advance_attention",
    )(*terms, *qkv, *out)


def waiting(kernel, others):
    corners = [corner(v) for v in jax.tree.leaves(others)]
    count = len(corners)
    return lambda *refs: kernel(*refs[count:]), corners, [whole(v) for v in corners]


SMEM_SPEC = pl.BlockSpec(memory_space=pltpu.SMEM)
like = jax.ShapeDtypeStruct


def per_part(array, size, by_x):
    return pl.BlockSpec((size, array.shape[1]), lambda g: (g // 2 if by_x else g % 2, 0))


def attention_weights(weights, rows):
    parts_qk, parts_vo = weights
    specs = []
    for part in parts_qk:
        block = (1, part.shape[1], rows, part.shape[3])
        specs.append(pl.BlockSpec(block, lambda g: (g, 0, 0, 0)))
    for part in parts_vo:
        block = (*part.shape[:2], rows, part.shape[3])
        specs.append(pl.BlockSpec(block, lambda g: (0, 0, 0, 0)))
    return [*parts_qk, *parts_vo], specs


def params(mib):
    return pltpu.CompilerParams(vmem_limit_bytes=mib << 20)


def cost(giga_flops, mega_bytes, mega_exps):
    return pl.CostEstimate(
        flops=int(giga_flops * 1e9),
        bytes_accessed=int(mega_bytes * 1e6),
        transcendentals=int(mega_exps * 1e6),
    )


def attention_forward(place, x, weights, biases, half, mask, vec_rows, mix, rows):
    length = x.shape[0]
    pair = weights[0][0].shape[3]
    width = pair // 2
    last = mix is not None
    row = like((length, D), F32)
    outs = [
        like((2, length, 3 * width), BF),
        like((2, 8, length), F32),
        like((2, length, width), BF),
    ]
    tail = [row]
    scratch = [pltpu.VMEM((D, pair), BF), pltpu.VMEM((D, pair), BF)]
    operands, specs = attention_weights(weights, rows)
    operands += [place, x, biases, mask, vec_rows]
    specs += [
        SMEM_SPEC,
        whole(x),
        pl.BlockSpec((1, *biases.shape[1:]), lambda g: (half * 2 + g, 0, 0)),
        whole(mask),
        whole(vec_rows),
    ]
    if last:
        low = like((length, D), BF)
        tail = [row, low, row, like((length, 128), F32), like((D, length), BF)]
        operands.append(mix)
        specs.append(whole(mix))
        scratch.append(pltpu.VMEM((length, D), F32))
    return pl.pallas_call(
        functools.partial(attention_forward_kernel, rows, last, len(weights[0])),
        grid=(2,),
        in_specs=specs,
        out_specs=[per_group(o) for o in outs] + [whole(o) for o in tail],
        out_shape=outs + tail,
        scratch_shapes=scratch,
        compiler_params=params(18),
        cost_estimate=cost(4.5, 6.0, 3.1),
        name="attention_forward_last" if last else "attention_forward",
    )(*operands)


def attention_backward(place, x_t, gr, gr_t, weights, saved, mask, start, rows, last, others):
    length = gr.shape[0]
    pair = weights[0][0].shape[3]
    width = pair // 2
    across = len(weights[0])
    deep = weights[0][0].shape[1]
    qkv, lse, context = saved
    grad_qk = like((across, 2, deep, rows, pair), BF)
    grad_vo = like((2, across, deep, rows, pair), BF)
    outs = [
        grad_qk,
        grad_vo,
        like((2, 8, width), F32),
        like((length, D), BF if last else F32),
    ]
    scratch = [
        pltpu.VMEM((D, pair), BF),
        pltpu.VMEM((D, pair), BF),
        pltpu.VMEM((length, 3 * width), BF),
    ]
    if last:
        scratch.append(pltpu.VMEM((length, D), F32))
    operands, specs = attention_weights(weights, rows)
    kernel = functools.partial(attention_backward_kernel, rows, last, across)
    kernel, corners, corner_specs = waiting(kernel, others)
    return pl.pallas_call(
        kernel,
        grid=(2,),
        in_specs=corner_specs
        + specs
        + [
            SMEM_SPEC,
            whole(x_t),
            whole(gr),
            whole(gr_t),
            per_group(qkv),
            per_group(lse),
            per_group(context),
            whole(mask),
            whole(start),
        ],
        out_specs=[
            per_corner(grad_qk, rows, 1),
            per_corner(grad_vo, rows, 0),
            per_group(outs[2]),
            whole(outs[3]),
        ],
        out_shape=outs,
        scratch_shapes=scratch,
        compiler_params=params(18),
        cost_estimate=cost(0.5, 1.0, 0.1),
        name="attention_backward_last" if last else "attention_backward",
    )(*corners, *operands, place, x_t, gr, gr_t, qkv, lse, context, mask, start)


def ffn_operands(up, down):
    chunk = up[0].shape[0] // 2
    specs = [per_part(u, chunk, False) for u in up] + [per_part(d, chunk, True) for d in down]
    return [*up, *down], specs, chunk


def ffn_forward(h, hb, up, down, bias, vec_rows, tail_operands):
    length = h.shape[0]
    operands, specs, chunk = ffn_operands(up, down)
    hidden = 4 * chunk
    last = len(tail_operands) > 0
    row = like((length, D), F32)
    outs = [like((length, hidden), BF), like((length, hidden), F32)]
    tail = [row]
    scratch = []
    if last:
        low = like((length, D), BF)
        tail = [low, row, low, like((8, D), F32)]
        scratch = [pltpu.VMEM((length, D), F32)]
    return pl.pallas_call(
        functools.partial(ffn_forward_kernel, last),
        grid=(4,),
        in_specs=specs
        + [whole(h), whole(hb), per_columns(bias, chunk), whole(vec_rows)]
        + [whole(t) for t in tail_operands],
        out_specs=[per_columns(o, chunk) for o in outs] + [whole(o) for o in tail],
        out_shape=outs + tail,
        scratch_shapes=scratch,
        compiler_params=params(18),
        cost_estimate=cost(4.9, 12.0, 1.6),
        name="ffn_forward_last" if last else "ffn_forward",
    )(*operands, h, hb, bias, vec_rows, *tail_operands)


def ffn_backward(grb, hb, act, slope, up, down, total, tail_operands, others):
    length = grb.shape[0]
    operands, specs, chunk = ffn_operands(up, down)
    hidden = 4 * chunk
    last = len(tail_operands) > 0
    row = like((length, D), F32)
    grad = like((hidden, D), BF)
    outs = [grad, grad, like((8, hidden), F32)]
    tail = [row]
    scratch = []
    if last:
        tail = [row, like((length, D), BF), like((D, length), BF), like((8, D), F32)]
        scratch = [pltpu.VMEM((length, D), F32)]
    kernel, corners, corner_specs = waiting(functools.partial(ffn_backward_kernel, last), others)
    return pl.pallas_call(
        kernel,
        grid=(4,),
        in_specs=corner_specs
        + specs
        + [whole(grb), whole(hb), per_columns(act, chunk), per_columns(slope, chunk)]
        + [whole(total)]
        + [whole(t) for t in tail_operands],
        out_specs=[
            per_rows(grad, chunk, False),
            per_rows(grad, chunk, True),
            per_columns(outs[2], chunk),
        ]
        + [whole(o) for o in tail],
        out_shape=outs + tail,
        scratch_shapes=scratch,
        compiler_params=params(18),
        cost_estimate=cost(9.7, 16.0, 0.0),
        name="ffn_backward_last" if last else "ffn_backward",
    )(*corners, *operands, grb, hb, act, slope, total, *tail_operands)


def advance(weight, grad, moment, average, decay, rate):
    step_grad = grad + decay * weight
    moment_new = MOMENTUM * moment + step_grad
    weight_new = weight - rate * (step_grad + MOMENTUM * moment_new)
    average_new = AVERAGE * average + (1.0 - AVERAGE) * weight_new
    return (weight_new, moment_new, average_new)


def body(
    layer_input,
    lengths,
    cotangent,
    w_qkv,
    w_out,
    w_up,
    w_down,
    vectors,
    mom_qkv,
    mom_out,
    mom_up,
    mom_down,
    mom_vec,
    avg_qkv,
    avg_out,
    avg_up,
    avg_down,
    avg_vec,
):
    z, x, y, c = (lax.axis_index(a) for a in ("z", "x", "y", "c"))
    deep = lax.axis_size("z")
    blocks = deep * 8
    rows, head_cols = w_qkv.shape[1], w_qkv.shape[2]
    pair = 2 * head_cols
    vec_len = vectors.shape[0]
    ff_rows = w_up.shape[1]
    local = layer_input.shape[0]
    length = 4 * local

    kc, kx, ky, kz = jnp.meshgrid(
        jnp.arange(2), jnp.arange(2), jnp.arange(2), z_order(deep), indexing="ij"
    )
    owner = (((z ^ kz) * 2 + (x ^ kx)) * 4 + (y ^ ky) * 2 + (c ^ kc)).reshape(blocks)
    tz, tx, ty, tc = jnp.meshgrid(
        jnp.arange(deep), jnp.arange(2), jnp.arange(2), jnp.arange(2), indexing="ij"
    )
    seat = ((((c ^ tc) * 2 + (x ^ tx)) * 2 + (y ^ ty)) * deep + z_order(deep)[z ^ tz]).reshape(blocks)
    first, second = jnp.meshgrid(jnp.arange(2), jnp.arange(2), indexing="ij")
    group_head = ((y ^ second) * 2 + (c ^ first)).reshape(4)
    head_group = ((c ^ second) * 2 + (y ^ first)).reshape(4)

    in_kernel = rows % 32 == 0 and deep == COUNTS[3]
    owner, group_head = owner.astype(jnp.int32), group_head.astype(jnp.int32)

    vec_row = jnp.pad(vectors.astype(BF), (0, pair - vec_len))[None]
    vec_rows = jnp.pad(jnp.concatenate([vec_row, send(vec_row, "c")], 0), ((0, 6), (0, 0)))
    pack_qk = jnp.concatenate([w_qkv[0], w_qkv[1]], 1).astype(BF)
    pack_vo = jnp.concatenate([w_qkv[2], w_out.T], 1).astype(BF)
    pack = jnp.concatenate([pack_qk, vec_rows, pack_vo], 0)
    doc_x, x_y = to_documents(after(layer_input, vec_rows))
    doc_cot, cot_y = to_documents(after(cotangent, vec_rows))
    attn_z, z_first = gather_z(pack)
    qk, vo = attn_z[:, : rows + 8], attn_z[:, rows + 8 :]
    qk_first, vo_first = send(qk, "y"), send(vo, "x")
    qk = after(jnp.stack([qk, qk_first], 0), vo_first, x_y, cot_y)
    vo = after(jnp.stack([vo, vo_first], 0), qk_first)
    qk_got, vo_got = send(qk, "x"), send(vo, "y")
    attn_own = ((qk, qk_got), (vo, vo_got))
    attn_other = jax.tree.map(lambda v: send(v, "c"), attn_own)

    pack = jnp.concatenate([w_up.T.astype(BF), w_down.astype(BF)], 0)
    ffn_z, _ = gather_z(after(pack, z_first))
    first_got = (qk_first, vo_first)
    up, down = after((ffn_z[:, :ff_rows], ffn_z[:, ff_rows:]), first_got)
    up_got, down_got = send(up, "y"), send(down, "x")
    up, down = (
        after(jnp.stack([up, up_got], 0), down_got, qk_got, vo_got),
        after(jnp.stack([down, down_got], 0), up_got, qk_got, vo_got),
    )
    up_got, down_got = send(up, "x"), send(down, "y")

    pieces = jnp.stack([qk[..., rows:, :], qk_got[..., rows:, :]], 0).astype(F32)
    if in_kernel:
        vec_rows, bias_up, biases = spread_vectors(owner, group_head, pieces, ff_rows, head_cols)
    else:
        vec_all = jnp.moveaxis(pieces[..., :2, :vec_len], -2, 0).reshape(blocks, vec_len)
        vec_rows = jnp.take(vec_all, seat, axis=0).reshape(12, D)
        bias_up = jnp.take(vec_rows[5:9].reshape(blocks, ff_rows), owner, axis=0)
        bias_up = jnp.pad(bias_up.reshape(2, 1, FF // 2), ((0, 0), (0, 7), (0, 0)))
        bias_q = jnp.take(vec_rows[0].reshape(4, head_cols), group_head, axis=0)
        bias_v = jnp.take(vec_rows[1].reshape(4, head_cols), group_head, axis=0)
        biases = jnp.pad(jnp.stack([bias_q, bias_v], 1), ((0, 0), (0, 6), (0, 0)))

    row = jnp.arange(length)
    part = row // local
    position = ((y ^ (part % 2)) * 2 + (c ^ (part // 2))) * local + row % local
    doc_len = lax.dynamic_index_in_dim(lengths, y * 2 + c, 0, keepdims=False)
    alive = position < doc_len
    mask = jnp.where(alive, 0.0, -1e30).astype(F32)
    mask_row = jnp.broadcast_to(mask[None, :], (8, length))
    mask_col = jnp.broadcast_to(mask[:, None], (length, 128))

    if in_kernel:
        zs = flip_order("z")[None, :]
        place = (zs * 2 + (x ^ jnp.arange(2)[:, None])).reshape(2 * deep)
        kernel_rows = rows
    else:
        xs = x ^ jnp.arange(2)
        zs = flip_order("z")

        def true_order(weights):
            qk, vo = (jnp.stack(parts, 0)[..., :rows, :] for parts in weights)
            qk = jnp.take(jnp.take(qk, xs, axis=0), zs, axis=2).transpose(1, 2, 0, 3, 4)
            vo = jnp.take(jnp.take(vo, xs, axis=1), zs, axis=2).transpose(0, 2, 1, 3, 4)
            qk, vo = qk.reshape(2, 1, D, pair), vo.reshape(2, 1, 1, D, pair)
            return ((qk,), (vo[0], vo[1]))

        def relative_order(qk, vo):
            qk = qk.reshape(2, deep, 2, rows, pair).transpose(2, 0, 1, 3, 4)
            vo = vo.reshape(2, deep, 2, rows, pair).transpose(0, 2, 1, 3, 4)
            qk = jnp.take(jnp.take(qk, xs, axis=0), zs, axis=2)
            return qk, jnp.take(jnp.take(vo, xs, axis=1), zs, axis=2)

        place = jnp.zeros((1,), jnp.int32)
        attn_own, attn_other = true_order(attn_own), true_order(attn_other)
        kernel_rows = D
    place = place.astype(jnp.int32)

    *saved_0, mix = attention_forward(
        place, doc_x, attn_own, biases, 0, mask_row, vec_rows, None, kernel_rows
    )
    *saved_1, hidden, hidden_b, normed, inverse, x_t = attention_forward(
        place, doc_x, attn_other, biases, 1, mask_row, vec_rows, mix, kernel_rows
    )
    flat = lambda v: v.reshape(FF // 4, D)
    up_own, down_own = (flat(up), flat(up_got)), (flat(down), flat(down_got))
    up_other = (send(up_own[0], "c"), send(after(up_own[1], hidden_b), "c"))
    down_other = (send(down_own[0], "c"), send(after(down_own[1], hidden_b), "c"))
    act_0, slope_0, mix = ffn_forward(
        hidden, hidden_b, up_own, down_own, bias_up[0], vec_rows, ()
    )
    act_1, slope_1, result, d_second, d_second_b, vec_two = ffn_forward(
        hidden, hidden_b, up_other, down_other, bias_up[1], vec_rows, (mix, doc_cot, mask_col)
    )
    out_own, out_y = from_documents_y(result, local)

    lead = (2, 2, deep, ff_rows, D)
    up_1, down_1, d_bias_1, d_hidden = ffn_backward(
        d_second_b, hidden_b, act_1, slope_1, up_other, down_other, d_second, (), ()
    )
    up_1, down_1 = send(up_1, "c"), send(down_1, "c")
    up_0, down_0, d_bias_0, d_first, d_first_b, d_first_t, vec_one = ffn_backward(
        d_second_b,
        hidden_b,
        act_0,
        slope_0,
        up_own,
        down_own,
        d_hidden,
        (normed, inverse, vec_rows),
        (out_y,),
    )
    grad_up = swap([up_0.reshape(lead), up_1.reshape(lead)], "x")
    grad_down = swap([down_0.reshape(lead), down_1.reshape(lead)], "y")
    ffn_c = (up_1, down_1)
    ffn_big = (grad_up[-1], grad_down[-1])
    grad_up, grad_down = swap(grad_up, "y"), swap(grad_down, "x")
    ffn_second = (grad_up[-1], grad_down[-1])
    grad_ffn = scatter_z([grad_up, grad_down])

    qk_1, vo_1, bias_1, d_attn = attention_backward(
        place, x_t, d_first_b, d_first_t, attn_other, saved_1, mask_col, d_first, kernel_rows, False, ffn_c
    )
    qk_0, vo_0, bias_0, d_input = attention_backward(
        place, x_t, d_first_b, d_first_t, attn_own, saved_0, mask_col, d_attn, kernel_rows, True, ()
    )
    if not in_kernel:
        qk_1, vo_1 = relative_order(qk_1, vo_1)
        qk_0, vo_0 = relative_order(qk_0, vo_0)
    qk_1, vo_1 = send(qk_1, "c"), send(vo_1, "c")

    bias_0 = after(bias_0, ffn_big)
    if in_kernel:
        vec_part = collect_vectors(
            owner, group_head, ff_rows, pair, bias_0, bias_1, d_bias_0, d_bias_1, vec_one, vec_two
        ).reshape(2, 2, 2, deep, 8, pair)
    else:
        d_bias = jnp.concatenate([bias_0, bias_1], 0)
        d_bias_q = jnp.take(d_bias[:, 0], head_group, axis=0).reshape(D)
        d_bias_v = jnp.take(d_bias[:, 1], head_group, axis=0).reshape(D)
        d_bias_up = jnp.concatenate([d_bias_0[0], d_bias_1[0]]).reshape(blocks, ff_rows)
        d_bias_up = jnp.take(d_bias_up, seat, axis=0).reshape(FF)
        grad_vec = jnp.concatenate(
            [
                d_bias_q,
                d_bias_v,
                vec_one[2],
                vec_one[0],
                vec_one[1],
                d_bias_up,
                vec_two[2],
                vec_two[0],
                vec_two[1],
            ]
        )
        vec_part = jnp.take(grad_vec.reshape(blocks, vec_len), owner, axis=0)
        vec_part = jnp.pad(vec_part, ((0, 0), (0, pair - vec_len))).reshape(2, 2, 2, deep, 1, pair)
        vec_part = jnp.pad(vec_part, ((0, 0),) * 4 + ((0, 7), (0, 0)))
    vec_part = vec_part[0] + send(vec_part[1], "c")
    sum_qk, vec_terms, sum_vo = [qk_0, qk_1], [vec_part], [vo_0, vo_1]
    for axis_qk, axis_vo in (("x", "y"), ("y", "x")):
        part = jnp.concatenate(
            [total([t[1] for t in sum_qk]), total([t[1] for t in vec_terms])], -2
        )
        got = send(after(part, ffn_second).astype(BF), axis_qk)
        sum_qk = [t[0] for t in sum_qk] + [got[..., :rows, :]]
        vec_terms = [t[0] for t in vec_terms] + [got[..., rows:, :]]
        sum_vo = swap(sum_vo, axis_vo, ffn_second)
    d_input = after(d_input, got, sum_vo[-1])
    grad_ffn = after(total(grad_ffn), got, sum_vo[-1])
    grad_up, grad_down = grad_ffn[:ff_rows].T, grad_ffn[ff_rows:]
    grad_attn = scatter_z([sum_qk, vec_terms, sum_vo])
    layer_output = from_documents(group_head, after(out_own, grad_ffn), out_y, BF)
    grad_input = from_documents(group_head, *from_documents_y(d_input, local), F32)

    slots = length * layer_input.shape[1] * deep * 2
    rate = RATE_BASE / math.sqrt(slots)
    rate_out = rate * math.sqrt(LEN / 8.0)
    olds_qkv, olds_out = (w_qkv, mom_qkv, avg_qkv), (w_out, mom_out, avg_out)
    if in_kernel:
        (
            grad_qkv,
            new_qkv,
            new_mom_qkv,
            new_avg_qkv,
            grad_out,
            new_out,
            new_mom_out,
            new_avg_out,
            grad_vec,
        ) = advance_attention(grad_attn, olds_qkv, olds_out, (rate, rate_out))
        grad_vec = grad_vec[0, :vec_len]
    else:
        grad_attn = total(grad_attn)
        sum_qk, sum_vo = grad_attn[:rows], grad_attn[rows + 8 :]
        grad_qkv = jnp.stack([sum_qk[:, :head_cols], sum_qk[:, head_cols:], sum_vo[:, :head_cols]])
        grad_out = sum_vo[:, head_cols:].T
        grad_vec = grad_attn[rows, :vec_len]
        new_qkv, new_mom_qkv, new_avg_qkv = advance(
            w_qkv, grad_qkv, mom_qkv, avg_qkv, DECAY, rate
        )
        new_out, new_mom_out, new_avg_out = advance(
            w_out, grad_out, mom_out, avg_out, DECAY, rate_out
        )
    new_up, new_mom_up, new_avg_up = advance(w_up, grad_up, mom_up, avg_up, DECAY, rate)
    new_down, new_mom_down, new_avg_down = advance(
        w_down, grad_down, mom_down, avg_down, DECAY, rate
    )
    new_vec, new_mom_vec, new_avg_vec = advance(vectors, grad_vec, mom_vec, avg_vec, 0.0, rate)
    return (
        layer_output,
        grad_input,
        grad_qkv,
        grad_out,
        grad_up,
        grad_down,
        grad_vec,
        new_qkv,
        new_out,
        new_up,
        new_down,
        new_vec,
        new_mom_qkv,
        new_mom_out,
        new_mom_up,
        new_mom_down,
        new_mom_vec,
        new_avg_qkv,
        new_avg_out,
        new_avg_up,
        new_avg_down,
        new_avg_vec,
    )


def solution(mesh):
    dp, head = mesh.shape["dp"], mesh.shape["head"]
    fine = Mesh(mesh.devices.reshape(dp // 2, 2, head // 2, 2), ("z", "x", "y", "c"))
    dps, heads, every = ("z", "x"), ("y", "c"), ("z", "x", "y", "c")
    acts = P(heads, dps, None)
    weights = (P(None, dps, heads), P(heads, dps), P(None, every), P(every, None), P(every))
    return jax.shard_map(
        body,
        mesh=fine,
        in_specs=(acts, P(dps), acts) + weights * 3,
        out_specs=(acts, acts) + weights * 4,
        check_vma=False,
    )
```

profile of v0, /device:TPU:0, one launch (start us, length us, event | category | flops | bytes accessed | tf_op | source)
XLA Modules:
  0.0 270.9 jit_solution(9589818093447183963)
XLA Ops:
  7.8 3.7 %collective-permute-start.1 = (bf16[200,384]{1,0:T(8,128)(2,1)S(1)}, bf16[200,384]{1,0:T(8,128)(2,1)S(1)}, u32[]{:S(2)}, u32[]{:S(2)}) collective-permute-start(bf16[200,384]{1,0:T(8,128)(2,1)S(1)} %maximum_maximum_fusion), channel_id=1, source_target_pairs={{0,16},{8,24},{16,0},{24,8},{1,17},{9,25},{17,1},{25,9},{2,18},{10... | collective-permute-start | bytes 460808 | tf_op jit(solution)/shard_map/ppermute | solution.py:30
  13.4 1.6 collective-permute-start.9
  15.9 3.4 %collective-permute-done.1 = bf16[200,384]{1,0:T(8,128)(2,1)S(1)} collective-permute-done((bf16[200,384]{1,0:T(8,128)(2,1)S(1)}, bf16[200,384]{1,0:T(8,128)(2,1)S(1)}, u32[]{:S(2)}, u32[]{:S(2)}) %collective-permute-start.1) | collective-permute-done | bytes 153632 | tf_op jit(solution)/shard_map/ppermute | solution.py:30
  21.4 3.4 %collective-permute-start.2 = (bf16[192,768]{1,0:T(8,128)(2,1)S(1)}, bf16[192,768]{1,0:T(8,128)(2,1)S(1)}, u32[]{:S(2)}, u32[]{:S(2)}) collective-permute-start(bf16[192,768]{1,0:T(8,128)(2,1)S(1)} %maximum_add_fusion.8), channel_id=1, source_target_pairs={{0,16},{8,24},{16,0},{24,8},{1,17},{9,25},{17,1},{25,9},{2,18},{10... | collective-permute-start | bytes 884744 | tf_op jit(solution)/shard_map/ppermute | solution.py:30
  25.5 7.7 %collective-permute-done.10 = bf16[2,128,768]{2,1,0:T(8,128)(2,1)S(1)} collective-permute-done((bf16[2,128,768]{2,1,0:T(8,128)(2,1)S(1)}, bf16[2,128,768]{2,1,0:T(8,128)(2,1)S(1)}, u32[]{:S(2)}, u32[]{:S(2)}) %collective-permute-start.10) | collective-permute-done | bytes 393248 | tf_op jit(solution)/shard_map/ppermute | solution.py:30
  35.7 2.5 collective-permute-done.2
  41.7 4.9 %collective-permute-done.6 = bf16[4,96,384]{2,1,0:T(8,128)(2,1)S(1)} collective-permute-done((bf16[4,96,384]{2,1,0:T(8,128)(2,1)S(1)}, bf16[4,96,384]{2,1,0:T(8,128)(2,1)S(1)}, u32[]{:S(2)}, u32[]{:S(2)}) %collective-permute-start.6) | collective-permute-done | bytes 294944 | tf_op jit(solution)/shard_map/ppermute | solution.py:30
  54.6 12.5 %collective-permute-done.12.refs_3_ = bf16[2,4,96,384]{3,2,1,0:T(8,128)(2,1)S(1)} collective-permute-done((bf16[2,4,96,384]{3,2,1,0:T(8,128)(2,1)S(1)}, bf16[2,4,96,384]{3,2,1,0:T(8,128)(2,1)S(1)}, u32[]{:S(2)}, u32[]{:S(2)}) %collective-permute-start.12) | collective-permute-done | bytes 589856 | tf_op jit(solution)/shard_map/ppermute | solution.py:30
  71.8 5.0 %collective-permute-done.7 = bf16[4,96,768]{2,1,0:T(8,128)(2,1)S(1)} collective-permute-done((bf16[4,96,768]{2,1,0:T(8,128)(2,1)S(1)}, bf16[4,96,768]{2,1,0:T(8,128)(2,1)S(1)}, u32[]{:S(2)}, u32[]{:S(2)}) %collective-permute-start.7) | collective-permute-done | bytes 589856 | tf_op jit(solution)/shard_map/ppermute | solution.py:30
  82.1 6.8 %attention_forward.1 = (bf16[2,512,576]{2,1,0:T(8,128)(2,1)S(1)}, f32[2,8,512]{2,1,0:T(8,128)S(1)}, bf16[2,512,192]{2,1,0:T(8,128)(2,1)S(1)}, f32[512,768]{1,0:T(8,128)S(1)}) custom-call(bf16[2,4,104,384]{3,2,1,0:T(8,128)(2,1)S(1)} %maximum_add_fusion.3.refs_0_, bf16[2,4,104,384]{3,2,1,0:T(8,128)(2,1)S(1)} %collective-permute-done.11.refs_1_, ...), custom_call_target="tpu_custom_call" | custom-call | flops 4499999744 | bytes 6000000 | tf_op jit(solution)/shard_map/attention_forward/pallas_call | solution.py:587
  89.6 7.2 %attention_forward_last.1 = (bf16[2,512,576]{2,1,0:T(8,128)(2,1)S(1)}, f32[2,8,512]{2,1,0:T(8,128)S(1)}, bf16[2,512,192]{2,1,0:T(8,128)(2,1)S(1)}, f32[512,768]{...) custom-call(bf16[2,4,104,384]{3,2,1,0:T(8,128)(2,1)S(1)} %collective, ...), custom_call_target="tpu_custom_call" | custom-call | flops 4499999744 | bytes 6000000 | tf_op jit(solution)/shard_map/attention_forward_last/pallas_call | solution.py:587
  98.0 8.6 %collective-permute-done.22 = bf16[2,4,96,768]{3,2,1,0:T(8,128)(2,1)S(1)} collective-permute-done((bf16[2,4,96,768]{3,2,1,0:T(8,128)(2,1)S(1)}, bf16[2,4,96,768]{3,2,1,0:T(8,128)(2,1)S(1)}, u32[]{:S(2)}, u32[]{:S(2)}) %collective-permute-start.22) | collective-permute-done | bytes 1179680 | tf_op jit(solution)/shard_map/ppermute | solution.py:30
  106.8 2.4 collective-permute-done.14
  109.5 6.4 %ffn_forward.1 = (bf16[512,1536]{1,0:T(8,128)(2,1)S(1)}, f32[512,1536]{1,0:T(8,128)S(1)}, f32[512,768]{1,0:T(8,128)S(1)}) custom-call(bf16[768,768]{1,0:T(8,128)(2,1)S(1)} %bitcast.425, bf16[768,768]{1,0:T(8,128)(2,1)S(1)} %bitcast.427, bf16[768,768]{1,0:T(8,128)(2,1)S(1)} %bitcast.420, bf16[768,768]{1,0:T(8,128)(2,1)S(1)} %bitcast.422, ...), custom_call_target="tpu_custom_call" | custom-call | flops 4899999744 | bytes 12000000 | tf_op jit(solution)/shard_map/ffn_forward/pallas_call | solution.py:674
  116.0 1.7 copy-done.13
  117.8 8.1 %ffn_forward_last.1 = (bf16[512,1536]{1,0:T(8,128)(2,1)S(1)}, f32[512,1536]{1,0:T(8,128)S(1)}, bf16[512,768]{1,0:T(8,128)(2,1)S(1)}, f32[512,768]{1,0:T(8,128)S(...) custom-call(bf16[768,768]{1,0:T(8,128)(2,1)S(1)} %collective-permute-done.13.refs_0_, ...), custom_call_target="tpu_custom_call" | custom-call | flops 4899999744 | bytes 12000000 | tf_op jit(solution)/shard_map/ffn_forward_last/pallas_call | solution.py:674
  125.9 1.6 copy-done.11
  127.5 1.9 copy-done.12
  129.4 7.5 %ffn_backward.1 = (bf16[1536,768]{1,0:T(8,128)(2,1)S(1)}, bf16[1536,768]{1,0:T(8,128)(2,1)S(1)}, f32[8,1536]{1,0:T(8,128)S(1)}, f32[512,768]{1,0:T(8,128)S(1)}) custom-call(bf16[768,768]{1,0:T(8,128)(2,1)S(1)} %collective-permute-done.13.refs_0_, bf16[768,768]{1,0:T(8,128)(2,1)S(1)} %collective-permute-done.20.refs_1_, ...), custom_call_target="tpu_custom_call" | custom-call | flops 9699999744 | bytes 16000000 | tf_op jit(solution)/shard_map/ffn_backward/pallas_call | solution.py:703
  138.2 11.0 %collective-permute-done.25.got_y_ref = bf16[2,128,768]{2,1,0:T(8,128)(2,1)S(1)} collective-permute-done((bf16[2,128,768]{2,1,0:T(8,128)(2,1)S(1)}, bf16[2,128,768]{2,1,0:T(8,128)(2,1)S(1)}, u32[]{:S(2)}, u32[]{:S(2)}) %collective-permute-start.25) | collective-permute-done | bytes 393248 | tf_op jit(solution)/shard_map/ppermute | solution.py:30
  149.2 2.0 copy-done.14
  151.2 8.7 %ffn_backward_last.1 = (bf16[1536,768]{1,0:T(8,128)(2,1)S(1)}, bf16[1536,768]{1,0:T(8,128)(2,1)S(1)}, f32[8,1536]{1,0:T(8,128)S(1)}, f32[512,768]{1,0:T(8,128)S(...) custom-call(bf16[8,128]{1,0:T(8,128)(2,1)S(1)} %slice_bitcast_fusion.67.refs_0_, ...), custom_call_target="tpu_custom_call" | custom-call | flops 9699999744 | bytes 16000000 | tf_op jit(solution)/shard_map/ffn_backward_last/pallas_call | solution.py:703
  159.9 1.6 add_convert_fusion.1
  164.7 11.2 %attention_backward.1 = (bf16[2,2,4,96,384]{4,3,2,1,0:T(8,128)(2,1)S(1)}, bf16[2,2,4,96,384]{4,3,2,1,0:T(8,128)(2,1)S(1)}, f32[2,8,192]{2,1,0:T(8,128)S(1)}, f32[512,768]{1,0:T(8,128)S(1)}) custom-call(bf16[8,128]{1,0:T(8,128)(2,1)S(1)} %slice_bitcast_fusion.66.refs_0_, bf16[8,128]{1,0:T(8,128)(2,1)S(1)} %slice_bitcast_fusion.65.refs_1_, ...), custom_call_target="tpu_custom_call" | custom-call | flops 500000000 | bytes 1000000 | tf_op jit(solution)/shard_map/attention_backward/pallas_call | solution.py:625
  177.5 11.3 %attention_backward_last.1 = (bf16[2,2,4,96,384]{4,3,2,1,0:T(8,128)(2,1)S(1)}, bf16[2,2,4,96,384]{4,3,2,1,0:T(8,128)(2,1)S(1)}, f32[2,8,192]{2,1,0:T(8,128)S(1)}, bf16[512,768]{1,0:T(8,128)(2,1)S(1)}) custom-call(bf16[2,4,104,384]{3,2,1,0:T(8,128)(2,1)S(1)} %maximum_add_fusion.3.refs_0_, bf16[2,4,104,384]{3,2,1,0:T(8,128)(2,1)S(1)} %collective-permute-done.11.refs_1_, ...), custom_call_target="tpu_custom_call" | custom-call | flops 500000000 | bytes 1000000 | tf_op jit(solution)/shard_map/attention_backward_last/pallas_call | solution.py:625
  197.8 8.2 %collective-permute-done.28 = bf16[4,96,768]{2,1,0:T(8,128)(2,1)S(1)} collective-permute-done((bf16[4,96,768]{2,1,0:T(8,128)(2,1)S(1)}, bf16[4,96,768]{2,1,0:T(8,128)(2,1)S(1)}, u32[]{:S(2)}, u32[]{:S(2)}) %collective-permute-start.28) | collective-permute-done | bytes 589856 | tf_op jit(solution)/shard_map/ppermute | solution.py:30
  212.9 10.3 %collective-permute-done.39 = bf16[2,4,96,384]{3,2,1,0:T(8,128)(2,1)S(1)} collective-permute-done((bf16[2,4,96,384]{3,2,1,0:T(8,128)(2,1)S(1)}, bf16[2,4,96,384]{3,2,1,0:T(8,128)(2,1)S(1)}, u32[]{:S(2)}, u32[]{:S(2)}) %collective-permute-start.39) | collective-permute-done | bytes 589856 | tf_op jit(solution)/shard_map/ppermute | solution.py:30
  227.3 2.2 collective-permute-start.33
  234.2 3.2 %collective-permute-done.37 = bf16[4,104,384]{2,1,0:T(8,128)(2,1)S(1)} collective-permute-done((bf16[4,104,384]{2,1,0:T(8,128)(2,1)S(1)}, bf16[4,104,384]{2,1,0:T(8,128)(2,1)S(1)}, u32[]{:S(2)}, u32[]{:S(2)}) %collective-permute-start.37) | collective-permute-done | bytes 319520 | tf_op jit(solution)/shard_map/ppermute | solution.py:30
  249.6 4.7 %collective-permute-done.44 = bf16[2,200,384]{2,1,0:T(8,128)(2,1)S(1)} collective-permute-done((bf16[2,200,384]{2,1,0:T(8,128)(2,1)S(1)}, bf16[2,200,384]{2,1,0:T(8,128)(2,1)S(1)}, u32[]{:S(2)}, u32[]{:S(2)}) %collective-permute-start.44) | collective-permute-done | bytes 307232 | tf_op jit(solution)/shard_map/ppermute | solution.py:30
  260.6 5.0 %collective-permute-done.45.refs_1_ = bf16[200,384]{1,0:T(8,128)(2,1)S(1)} collective-permute-done((bf16[200,384]{1,0:T(8,128)(2,1)S(1)}, bf16[200,384]{1,0:T(8,128)(2,1)S(1)}, u32[]{:S(2)}, u32[]{:S(2)}) %collective-permute-start.45) | collective-permute-done | bytes 153632 | tf_op jit(solution)/shard_map/ppermute | solution.py:30
  268.4 2.2 copy.62
  (315 shorter events, 78.2 us)
Async XLA Ops:
  7.8 11.6 %collective-permute-start.1 = (bf16[200,384]{1,0:T(8,128)(2,1)S(1)}, bf16[200,384]{1,0:T(8,128)(2,1)S(1)}, u32[]{:S(2)}, u32[]{:S(2)}) collective-permute-start(bf16[200,384]{1,0:T(8,128)(2,1)S(1)} %maximum_maximum_fusion), channel_id=1, source_target_pairs={{0,16},{8,24},{16,0},{24,8},{1,17},{9,25},{17,1},{25,9},{2,18},{10... | collective-permute-start | bytes 460808 | tf_op jit(solution)/shard_map/ppermute | solution.py:30
  13.4 12.0 %collective-permute-start.9 = (bf16[2,128,768]{2,1,0:T(8,128)(2,1)S(1)}, bf16[2,128,768]{2,1,0:T(8,128)(2,1)S(1)}, u32[]{:S(2)}, u32[]{:S(2)}) collective-permute-start(bf16[2,128,768]{2,1,0:T(8,128)(2,1)S(1)} %dynamic-slice_bitcast_fusion.1), channel_id=1, source_target_pairs={{0,2},{2,0},{1,3},{3,1},{4,6},{6,4},{5,7},{7,5},{8,10},{10,8},{9,1... | collective-permute-start | bytes 1179656 | tf_op jit(solution)/shard_map/ppermute | solution.py:30
  15.2 18.0 %collective-permute-start.10 = (bf16[2,128,768]{2,1,0:T(8,128)(2,1)S(1)}, bf16[2,128,768]{2,1,0:T(8,128)(2,1)S(1)}, u32[]{:S(2)}, u32[]{:S(2)}) collective-permute-start(bf16[2,128,768]{2,1,0:T(8,128)(2,1)S(1)} %dynamic-slice_bitcast_fusion), channel_id=1, source_target_pairs={{0,2},{2,0},{1,3},{3,1},{4,6},{6,4},{5,7},{7,5},{8,10},{10,8},{9,1... | collective-permute-start | bytes 1179656 | tf_op jit(solution)/shard_map/ppermute | solution.py:30
  19.4 18.9 %collective-permute-start.4 = (bf16[2,200,384]{2,1,0:T(8,128)(2,1)S(1)}, bf16[2,200,384]{2,1,0:T(8,128)(2,1)S(1)}, u32[]{:S(2)}, u32[]{:S(2)}) collective-permute-start(bf16[2,200,384]{2,1,0:T(8,128)(2,1)S(1)} %pad_maximum_fusion.10), channel_id=1, source_target_pairs={{0,8},{8,0},{16,24},{24,16},{1,9},{9,1},{17,25},{25,17},{2,10},{10... | collective-permute-start | bytes 921608 | tf_op jit(solution)/shard_map/ppermute | solution.py:30
  21.4 16.7 %collective-permute-start.2 = (bf16[192,768]{1,0:T(8,128)(2,1)S(1)}, bf16[192,768]{1,0:T(8,128)(2,1)S(1)}, u32[]{:S(2)}, u32[]{:S(2)}) collective-permute-start(bf16[192,768]{1,0:T(8,128)(2,1)S(1)} %maximum_add_fusion.8), channel_id=1, source_target_pairs={{0,16},{8,24},{16,0},{24,8},{1,17},{9,25},{17,1},{25,9},{2,18},{10... | collective-permute-start | bytes 884744 | tf_op jit(solution)/shard_map/ppermute | solution.py:30
  35.5 16.8 %collective-permute-start.19 = (bf16[2,128,768]{2,1,0:T(8,128)(2,1)S(1)}, bf16[2,128,768]{2,1,0:T(8,128)(2,1)S(1)}, u32[]{:S(2)}, u32[]{:S(2)}) collective-permute-start(bf16[2,128,768]{2,1,0:T(8,128)(2,1)S(1)} %pad_maximum_fusion.6), channel_id=1, source_target_pairs={{0,1},{1,0},{2,3},{3,2},{4,5},{5,4},{6,7},{7,6},{8,9},{9,8},{10,11... | collective-permute-start | bytes 1179656 | tf_op jit(solution)/shard_map/ppermute | solution.py:30
  38.3 14.7 %collective-permute-start.3 = (bf16[2,192,768]{2,1,0:T(8,128)(2,1)S(1)}, bf16[2,192,768]{2,1,0:T(8,128)(2,1)S(1)}, u32[]{:S(2)}, u32[]{:S(2)}) collective-permute-start(bf16[2,192,768]{2,1,0:T(8,128)(2,1)S(1)} %pad_maximum_fusion.4), channel_id=1, source_target_pairs={{0,8},{8,0},{16,24},{24,16},{1,9},{9,1},{17,25},{25,17},{2,10},{10... | collective-permute-start | bytes 1769480 | tf_op jit(solution)/shard_map/ppermute | solution.py:30
  48.7 20.9 %collective-permute-start.11 = (bf16[2,4,104,384]{3,2,1,0:T(8,128)(2,1)S(1)}, bf16[2,4,104,384]{3,2,1,0:T(8,128)(2,1)S(1)}, u32[]{:S(2)}, u32[]{:S(2)}) collective-permute-start(bf16[2,4,104,384]{3,2,1,0:T(8,128)(2,1)S(1)} %maximum_add_fusion.3.refs_0_), channel_id=1, source_target_pairs={{0,4},{4,0},{1,5},{5,1},{2,6},{6,2},{3,7},{7,3},{8,12},{12,8},{9,1... | collective-permute-start | bytes 1916936 | tf_op jit(solution)/shard_map/ppermute | solution.py:30
  50.8 16.3 %collective-permute-start.12 = (bf16[2,4,96,384]{3,2,1,0:T(8,128)(2,1)S(1)}, bf16[2,4,96,384]{3,2,1,0:T(8,128)(2,1)S(1)}, u32[]{:S(2)}, u32[]{:S(2)}) collective-permute-start(bf16[2,4,96,384]{3,2,1,0:T(8,128)(2,1)S(1)} %maximum_add_fusion.5.refs_2_), channel_id=1, source_target_pairs={{0,2},{2,0},{1,3},{3,1},{4,6},{6,4},{5,7},{7,5},{8,10},{10,8},{9,1... | collective-permute-start | bytes 1769480 | tf_op jit(solution)/shard_map/ppermute | solution.py:30
  52.4 36.5 %collective-permute-start.15 = (bf16[2,4,104,384]{3,2,1,0:T(8,128)(2,1)S(1)}, bf16[2,4,104,384]{3,2,1,0:T(8,128)(2,1)S(1)}, u32[]{:S(2)}, u32[]{:S(2)}) collective-permute-start(bf16[2,4,104,384]{3,2,1,0:T(8,128)(2,1)S(1)} %maximum_add_fusion.3.refs_0_), channel_id=1, source_target_pairs={{0,1},{1,0},{2,3},{3,2},{4,5},{5,4},{6,7},{7,6},{8,9},{9,8},{10,11... | collective-permute-start | bytes 1916936 | tf_op jit(solution)/shard_map/ppermute | solution.py:30
  52.4 28.6 %collective-permute-start.17 = (bf16[2,4,96,384]{3,2,1,0:T(8,128)(2,1)S(1)}, bf16[2,4,96,384]{3,2,1,0:T(8,128)(2,1)S(1)}, u32[]{:S(2)}, u32[]{:S(2)}) collective-permute-start(bf16[2,4,96,384]{3,2,1,0:T(8,128)(2,1)S(1)} %maximum_add_fusion.5.refs_2_), channel_id=1, source_target_pairs={{0,1},{1,0},{2,3},{3,2},{4,5},{5,4},{6,7},{7,6},{8,9},{9,8},{10,11... | collective-permute-start | bytes 1769480 | tf_op jit(solution)/shard_map/ppermute | solution.py:30
  53.2 23.6 %collective-permute-start.7 = (bf16[4,96,768]{2,1,0:T(8,128)(2,1)S(1)}, bf16[4,96,768]{2,1,0:T(8,128)(2,1)S(1)}, u32[]{:S(2)}, u32[]{:S(2)}) collective-permute-start(bf16[4,96,768]{2,1,0:T(8,128)(2,1)S(1)} %get-tuple-element.192), channel_id=1, source_target_pairs={{0,2},{2,0},{1,3},{3,1},{4,6},{6,4},{5,7},{7,5},{8,10},{10,8},{9,1... | collective-permute-start | bytes 1769480 | tf_op jit(solution)/shard_map/ppermute | solution.py:30
  69.6 19.4 %collective-permute-start.18 = (bf16[2,4,96,384]{3,2,1,0:T(8,128)(2,1)S(1)}, bf16[2,4,96,384]{3,2,1,0:T(8,128)(2,1)S(1)}, u32[]{:S(2)}, u32[]{:S(2)}) collective-permute-start(bf16[2,4,96,384]{3,2,1,0:T(8,128)(2,1)S(1)} %collective-permute-done.12.refs_3_), channel_id=1, source_target_pairs={{0,1},{1,0},{2,3},{3,2},{4,5},{5,4},{6,7},{7,6},{8,9},{9,8},{10,11... | collective-permute-start | bytes 1769480 | tf_op jit(solution)/shard_map/ppermute | solution.py:30
  76.8 12.7 %collective-permute-start.16 = (bf16[2,4,104,384]{3,2,1,0:T(8,128)(2,1)S(1)}, bf16[2,4,104,384]{3,2,1,0:T(8,128)(2,1)S(1)}, u32[]{:S(2)}, u32[]{:S(2)}) collective-permute-start(bf16[2,4,104,384]{3,2,1,0:T(8,128)(2,1)S(1)} %collective-permute-done.11.refs_1_), channel_id=1, source_target_pairs={{0,1},{1,0},{2,3},{3,2},{4,5},{5,4},{6,7},{7,6},{8,9},{9,8},{10,11... | collective-permute-start | bytes 1916936 | tf_op jit(solution)/shard_map/ppermute | solution.py:30
  78.1 28.4 %collective-permute-start.22 = (bf16[2,4,96,768]{3,2,1,0:T(8,128)(2,1)S(1)}, bf16[2,4,96,768]{3,2,1,0:T(8,128)(2,1)S(1)}, u32[]{:S(2)}, u32[]{:S(2)}) collective-permute-start(bf16[2,4,96,768]{3,2,1,0:T(8,128)(2,1)S(1)} %maximum_add_fusion.2), channel_id=1, source_target_pairs={{0,2},{2,0},{1,3},{3,1},{4,6},{6,4},{5,7},{7,5},{8,10},{10,8},{9,1... | collective-permute-start | bytes 3538952 | tf_op jit(solution)/shard_map/ppermute | solution.py:30
  81.0 28.2 %collective-permute-start.14 = (bf16[2,4,96,768]{3,2,1,0:T(8,128)(2,1)S(1)}, bf16[2,4,96,768]{3,2,1,0:T(8,128)(2,1)S(1)}, u32[]{:S(2)}, u32[]{:S(2)}) collective-permute-start(bf16[2,4,96,768]{3,2,1,0:T(8,128)(2,1)S(1)} %maximum_add_fusion.1), channel_id=1, source_target_pairs={{0,4},{4,0},{1,5},{5,1},{2,6},{6,2},{3,7},{7,3},{8,12},{12,8},{9,1... | collective-permute-start | bytes 3538952 | tf_op jit(solution)/shard_map/ppermute | solution.py:30
  88.9 20.5 %collective-permute-start.24 = (bf16[2,128,768]{2,1,0:T(8,128)(2,1)S(1)}, bf16[2,128,768]{2,1,0:T(8,128)(2,1)S(1)}, u32[]{:S(2)}, u32[]{:S(2)}) collective-permute-start(bf16[2,128,768]{2,1,0:T(8,128)(2,1)S(1)} %pad_maximum_fusion.7), channel_id=1, source_target_pairs={{0,1},{1,0},{2,3},{3,2},{4,5},{5,4},{6,7},{7,6},{8,9},{9,8},{10,11... | collective-permute-start | bytes 1179656 | tf_op jit(solution)/shard_map/ppermute | solution.py:30
  89.0 28.7 %collective-permute-start.21 = (bf16[768,768]{1,0:T(8,128)(2,1)S(1)}, bf16[768,768]{1,0:T(8,128)(2,1)S(1)}, u32[]{:S(2)}, u32[]{:S(2)}) collective-permute-start(bf16[768,768]{1,0:T(8,128)(2,1)S(1)} %bitcast.419), channel_id=1, source_target_pairs={{0,1},{1,0},{2,3},{3,2},{4,5},{5,4},{6,7},{7,6},{8,9},{9,8},{10,11... | collective-permute-start | bytes 3538952 | tf_op jit(solution)/shard_map/ppermute | solution.py:30
  89.5 28.2 %collective-permute-start.13 = (bf16[768,768]{1,0:T(8,128)(2,1)S(1)}, bf16[768,768]{1,0:T(8,128)(2,1)S(1)}, u32[]{:S(2)}, u32[]{:S(2)}) collective-permute-start(bf16[768,768]{1,0:T(8,128)(2,1)S(1)} %bitcast.424), channel_id=1, source_target_pairs={{0,1},{1,0},{2,3},{3,2},{4,5},{5,4},{6,7},{7,6},{8,9},{9,8},{10,11... | collective-permute-start | bytes 3538952 | tf_op jit(solution)/shard_map/ppermute | solution.py:30
  136.9 22.9 %collective-permute-start.26 = (bf16[1536,768]{1,0:T(8,128)(2,1)S(1)}, bf16[1536,768]{1,0:T(8,128)(2,1)}, u32[]{:S(2)}, u32[]{:S(2)}) collective-permute-start(bf16[1536,768]{1,0:T(8,128)(2,1)S(1)} %get-tuple-element.92), channel_id=1, source_target_pairs={{0,1},{1,0},{2,3},{3,2},{4,5},{5,4},{6,7},{7,6},{8,9},{9,8},{10,11... | collective-permute-start | bytes 7077896 | tf_op jit(solution)/shard_map/ppermute | solution.py:30
  137.5 25.1 %collective-permute-start.29 = (bf16[1536,768]{1,0:T(8,128)(2,1)S(1)}, bf16[1536,768]{1,0:T(8,128)(2,1)S(1)}, u32[]{:S(2)}, u32[]{:S(2)}) collective-permute-start(bf16[1536,768]{1,0:T(8,128)(2,1)S(1)} %get-tuple-element.94), channel_id=1, source_target_pairs={{0,1},{1,0},{2,3},{3,2},{4,5},{5,4},{6,7},{7,6},{8,9},{9,8},{10,11... | collective-permute-start | bytes 7077896 | tf_op jit(solution)/shard_map/ppermute | solution.py:30
  161.5 29.0 %collective-permute-start.27 = (bf16[2,4,96,768]{3,2,1,0:T(8,128)(2,1)S(1)}, bf16[2,4,96,768]{3,2,1,0:T(8,128)(2,1)S(1)}, u32[]{:S(2)}, u32[]{:S(2)}) collective-permute-start(bf16[2,4,96,768]{3,2,1,0:T(8,128)(2,1)S(1)} %bitcast.457), channel_id=1, source_target_pairs={{0,4},{4,0},{1,5},{5,1},{2,6},{6,2},{3,7},{7,3},{8,12},{12,8},{9,1... | collective-permute-start | bytes 3538952 | tf_op jit(solution)/shard_map/ppermute | solution.py:30
  162.9 28.8 %collective-permute-start.30 = (bf16[2,4,96,768]{3,2,1,0:T(8,128)(2,1)S(1)}, bf16[2,4,96,768]{3,2,1,0:T(8,128)(2,1)S(1)}, u32[]{:S(2)}, u32[]{:S(2)}) collective-permute-start(bf16[2,4,96,768]{3,2,1,0:T(8,128)(2,1)S(1)} %bitcast.456), channel_id=1, source_target_pairs={{0,2},{2,0},{1,3},{3,1},{4,6},{6,4},{5,7},{7,5},{8,10},{10,8},{9,1... | collective-permute-start | bytes 3538952 | tf_op jit(solution)/shard_map/ppermute | solution.py:30
  175.9 20.5 %collective-permute-start.34 = (bf16[2,2,4,96,384]{4,3,2,1,0:T(8,128)(2,1)S(1)}, bf16[2,2,4,96,384]{4,3,2,1,0:T(8,128)(2,1)S(1)}, u32[]{:S(2)}, u32[]{:S(2)}) collective-permute-start(bf16[2,2,4,96,384]{4,3,2,1,0:T(8,128)(2,1)S(1)} %get-tuple-element.107), channel_id=1, source_target_pairs={{0,1},{1,0},{2,3},{3,2},{4,5},{5,4},{6,7},{7,6},{8,9},{9,8},{10,11... | collective-permute-start | bytes 3538952 | tf_op jit(solution)/shard_map/ppermute | solution.py:30
  175.9 32.9 %collective-permute-start.38 = (bf16[2,2,4,96,384]{4,3,2,1,0:T(8,128)(2,1)S(1)}, bf16[2,2,4,96,384]{4,3,2,1,0:T(8,128)(2,1)S(1)}, u32[]{:S(2)}, u32[]{:S(2)}) collective-permute-start(bf16[2,2,4,96,384]{4,3,2,1,0:T(8,128)(2,1)S(1)} %get-tuple-element.115), channel_id=1, source_target_pairs={{0,1},{1,0},{2,3},{3,2},{4,5},{5,4},{6,7},{7,6},{8,9},{9,8},{10,11... | collective-permute-start | bytes 3538952 | tf_op jit(solution)/shard_map/ppermute | solution.py:30
  190.6 15.4 %collective-permute-start.28 = (bf16[4,96,768]{2,1,0:T(8,128)(2,1)S(1)}, bf16[4,96,768]{2,1,0:T(8,128)(2,1)S(1)}, u32[]{:S(2)}, u32[]{:S(2)}) collective-permute-start(bf16[4,96,768]{2,1,0:T(8,128)(2,1)S(1)} %fusion.2), channel_id=1, source_target_pairs={{0,2},{2,0},{1,3},{3,1},{4,6},{6,4},{5,7},{7,5},{8,10},{10,8},{9,1... | collective-permute-start | bytes 1769480 | tf_op jit(solution)/shard_map/ppermute | solution.py:30
  191.9 15.1 %collective-permute-start.31 = (bf16[4,96,768]{2,1,0:T(8,128)(2,1)S(1)}, bf16[4,96,768]{2,1,0:T(8,128)(2,1)S(1)}, u32[]{:S(2)}, u32[]{:S(2)}) collective-permute-start(bf16[4,96,768]{2,1,0:T(8,128)(2,1)S(1)} %fusion.1), channel_id=1, source_target_pairs={{0,4},{4,0},{1,5},{5,1},{2,6},{6,2},{3,7},{7,3},{8,12},{12,8},{9,1... | collective-permute-start | bytes 1769480 | tf_op jit(solution)/shard_map/ppermute | solution.py:30
  209.0 14.2 %collective-permute-start.39 = (bf16[2,4,96,384]{3,2,1,0:T(8,128)(2,1)S(1)}, bf16[2,4,96,384]{3,2,1,0:T(8,128)(2,1)S(1)}, u32[]{:S(2)}, u32[]{:S(2)}) collective-permute-start(bf16[2,4,96,384]{3,2,1,0:T(8,128)(2,1)S(1)} %fusion.4), channel_id=1, source_target_pairs={{0,2},{2,0},{1,3},{3,1},{4,6},{6,4},{5,7},{7,5},{8,10},{10,8},{9,1... | collective-permute-start | bytes 1769480 | tf_op jit(solution)/shard_map/ppermute | solution.py:30
  210.4 14.1 %collective-permute-start.32 = (bf16[2,192,768]{2,1,0:T(8,128)(2,1)S(1)}, bf16[2,192,768]{2,1,0:T(8,128)(2,1)S(1)}, u32[]{:S(2)}, u32[]{:S(2)}) collective-permute-start(bf16[2,192,768]{2,1,0:T(8,128)(2,1)S(1)} %pad_maximum_fusion.5), channel_id=1, source_target_pairs={{0,8},{8,0},{16,24},{24,16},{1,9},{9,1},{17,25},{25,17},{2,10},{10... | collective-permute-start | bytes 1769480 | tf_op jit(solution)/shard_map/ppermute | solution.py:30
  211.9 17.7 %collective-permute-start.36 = (bf16[2,4,104,384]{3,2,1,0:T(8,128)(2,1)S(1)}, bf16[2,4,104,384]{3,2,1,0:T(8,128)(2,1)S(1)}, u32[]{:S(2)}, u32[]{:S(2)}) collective-permute-start(bf16[2,4,104,384]{3,2,1,0:T(8,128)(2,1)S(1)} %fusion), channel_id=1, source_target_pairs={{0,4},{4,0},{1,5},{5,1},{2,6},{6,2},{3,7},{7,3},{8,12},{12,8},{9,1... | collective-permute-start | bytes 1916936 | tf_op jit(solution)/shard_map/ppermute | solution.py:30
  227.3 14.2 %collective-permute-start.33 = (bf16[192,768]{1,0:T(8,128)(2,1)}, bf16[192,768]{1,0:T(8,128)(2,1)}, u32[]{:S(2)}, u32[]{:S(2)}) collective-permute-start(bf16[192,768]{1,0:T(8,128)(2,1)} %pad_maximum_fusion.14), channel_id=1, source_target_pairs={{0,16},{8,24},{16,0},{24,8},{1,17},{9,25},{17,1},{25,9},{2,18},{10... | collective-permute-start | bytes 884744 | tf_op jit(solution)/shard_map/ppermute | solution.py:30
  246.1 12.1 %collective-permute-start.42 = (bf16[2,128,768]{2,1,0:T(8,128)(2,1)S(1)}, bf16[2,128,768]{2,1,0:T(8,128)(2,1)S(1)}, u32[]{:S(2)}, u32[]{:S(2)}) collective-permute-start(bf16[2,128,768]{2,1,0:T(8,128)(2,1)S(1)} %get-tuple-element.193), channel_id=1, source_target_pairs={{0,2},{2,0},{1,3},{3,1},{4,6},{6,4},{5,7},{7,5},{8,10},{10,8},{9,1... | collective-permute-start | bytes 1179656 | tf_op jit(solution)/shard_map/ppermute | solution.py:30
  (61 other events, 439.3 us)
where the time goes:
time: 276 us; the launch traced here: 271 us
  waiting for transfers between devices  95.6 us (35%)
  Pallas kernels  71.6 us (26%)
  starting transfers between devices  38.7 us (14%)
  other arithmetic  26.1 us (9%)
  local copies, waits for them, and re-layouts  24.7 us (9%)
  between operations  14.2 us (5%)
    ppermute x46, waiting for transfers between devices, send(): lax.ppermute(values, axis, [(i, i ^ bit) for i in range(lax.axis_size(axi...  95.6 us
    ppermute x46, starting transfers between devices, send(): lax.ppermute(values, axis, [(i, i ^ bit) for i in range(lax.axis_size(axi...  38.7 us
    pallas_call x2, Pallas kernels, attention_backward(): pl.pallas_call(kernel, grid=(2,), in_specs=corner_specs + specs + [SMEM_S...  22.5 us
    pallas_call x2, Pallas kernels, ffn_backward(): pl.pallas_call(kernel, grid=(4,), in_specs=corner_specs + specs + [whole(...  16.2 us
    pallas_call x2, Pallas kernels, ffn_forward(): pl.pallas_call(functools.partial(ffn_forward_kernel, last), grid=(4,), in...  14.5 us
    pallas_call x2, Pallas kernels, attention_forward(): pl.pallas_call(functools.partial(attention_forward_kernel, rows, last, le...  14 us
    unnamed x95, local copies, waits for them, and re-layouts  13 us
    slice x18, local copies, waits for them, and re-layouts, after(): corner(v)[0, 0].astype(F32) * 0.0  9.3 us
  transfers between devices with their start and end apart: 46, of which 20 were waited for; matrix products, arithmetic and copies ran while one was open for 13% of the time, Pallas kernels for 20%

commit v1 on v0

--- a/solution.py
+++ b/solution.py
@@ -72,12 +72,15 @@
     return [t[0] for t in terms] + [got]
 
 
-def scatter_z(sums):
+def scatter_z(sums, direct):
     joined = lambda index: jnp.concatenate([total([t[index] for t in terms]) for terms in sums], -2)
     if lax.axis_size("z") != 4:
         everything = jnp.take(joined(slice(None)).astype(BF), flip_order("z"), axis=0)
         parts = lax.all_to_all(everything, "z", 0, 0, tiled=True)
-        return [total(list(parts[1:])), parts[0]]
+        return [total(list(parts[1:])), parts[0]], parts[0]
+    if direct:
+        parts = [joined(place).astype(BF) for place in (1, 2, 3)]
+        return [joined(0)] + [send(part, "z", bit) for part, bit in zip(parts, (2, 1, 3))], parts[2]
     got = send(joined(slice(2, 4)).astype(BF), "z", 1)
     left, start = [], 0
     for terms in sums:
@@ -85,7 +88,8 @@
         left.append([t[:2] for t in terms] + [got[:, start:end]])
         start = end
     sums = left
-    return [joined(0), send(joined(1).astype(BF), "z", 2)]
+    part = joined(1).astype(BF)
+    return [joined(0), send(part, "z", 2)], part
 
 
 def to_documents(values):
@@ -149,18 +153,13 @@
     return pl.multiple_of(start, 32) if rows % 32 == 0 else start
 
 
-def place_weights(place_ref, qk_refs, vo_refs, w_qk, w_vo, rows):
-    across, deep = len(qk_refs), qk_refs[0].shape[1]
-
-    def place(group):
-        for i in range(across):
-            for k in range(deep):
-                start = block_start(place_ref, i * deep + k, rows)
-                w_qk[pl.ds(start, rows), :] = qk_refs[i][0, k]
-                w_vo[pl.ds(start, rows), :] = vo_refs[group][i, k]
-
-    for group in range(2):
-        pl.when(pl.program_id(0) == group)(functools.partial(place, group))
+def place_weights(place_ref, qk_ref, vo_ref, w_qk, w_vo, rows):
+    across, _, deep = qk_ref.shape[:3]
+    for i in range(across):
+        for k in range(deep):
+            start = block_start(place_ref, i * deep + k, rows)
+            w_qk[pl.ds(start, rows), :] = qk_ref[i, 0, k]
+            w_vo[pl.ds(start, rows), :] = vo_ref[0, i, k]
 
 
 def accumulate(step, target, start_ref, value):
@@ -173,8 +172,8 @@
         target[...] += value
 
 
-def attention_forward_kernel(rows, last, parts, *refs):
-    qk_refs, vo_refs, refs = refs[:parts], refs[parts : parts + 2], refs[parts + 2 :]
+def attention_forward_kernel(rows, last, *refs):
+    qk_ref, vo_ref, *refs = refs
     place_ref, x_ref, bias_ref, mask_ref, vec_ref = refs[:5]
     if last:
         mix_in, qkv_ref, lse_ref, context_ref = refs[5:9]
@@ -183,7 +182,7 @@
         mix_in = None
         qkv_ref, lse_ref, context_ref, mix_ref, w_qk, w_vo = refs[5:]
     step = pl.program_id(0)
-    place_weights(place_ref, qk_refs, vo_refs, w_qk, w_vo, rows)
+    place_weights(place_ref, qk_ref, vo_ref, w_qk, w_vo, rows)
     x = x_ref[...]
     width = w_qk.shape[1] // 2
     bias = bias_ref[0]
@@ -228,8 +227,8 @@
             xt_ref[...] = x_ref[...].T
 
 
-def attention_backward_kernel(rows, last, parts, *refs):
-    qk_refs, vo_refs, refs = refs[:parts], refs[parts : parts + 2], refs[parts + 2 :]
+def attention_backward_kernel(rows, last, *refs):
+    qk_ref, vo_ref, *refs = refs
     place_ref, xt_ref, gr_ref, grt_ref, qkv_ref, lse_ref, context_ref = refs[:7]
     mask_ref, start_ref = refs[7:9]
     if last:
@@ -237,7 +236,7 @@
     else:
         gqk_ref, gvo_ref, bias_ref, gin_ref, w_qk, w_vo, g_qkv = refs[9:]
     step = pl.program_id(0)
-    place_weights(place_ref, qk_refs, vo_refs, w_qk, w_vo, rows)
+    place_weights(place_ref, qk_ref, vo_ref, w_qk, w_vo, rows)
     width = w_qk.shape[1] // 2
     gc = dot(gr_ref[...], w_vo[:, width:], NN).astype(BF)
     mask = mask_ref[:, :1]
@@ -302,7 +301,8 @@
     phi = 0.5 + 0.5 * lax.erf(u * 0.7071067811865476)
     act = (u * phi).astype(BF)
     act_ref[...] = act
-    slope_ref[...] = phi + u * jnp.exp(-0.5 * u * u) * 0.3989422804014327
+    slope = phi + u * jnp.exp(-0.5 * u * u) * 0.3989422804014327
+    slope_ref[...] = slope.astype(slope_ref.dtype)
     accumulate(step, sum_ref, sum_in, dot(act, down, NN))
     if last:
 
@@ -330,7 +330,7 @@
         gu_ref, gd_ref, bias_ref, sum_ref = refs[9:]
     step = pl.program_id(0)
     grb = grb_ref[...]
-    d_up = dot(grb, down, NT) * slope_ref[...]
+    d_up = dot(grb, down, NT) * slope_ref[...].astype(F32)
     bias_ref[0:1] = jnp.sum(d_up, 0, keepdims=True)
     d_up_b = d_up.astype(BF)
     gd_ref[...] = dot(act_ref[...].T, grb, NN).astype(BF)
@@ -377,7 +377,9 @@
     return pl.BlockSpec((array.shape[0], size), lambda g: (0, g))
 
 
-def spread_vectors_kernel(owner_ref, heads_ref, pieces_ref, rows_ref, up_ref, bias_ref, units):
+def spread_vectors_kernel(
+    owner_ref, heads_ref, own_ref, other_ref, rows_ref, up_ref, bias_ref, units
+):
     _, across, _, deep = COUNTS
     unit = units.shape[1]
     for x in range(2):
@@ -387,8 +389,8 @@
                     index = ((c * across + x) * 2 + y) * deep + z
                     start = owner_ref[index] * 3
                     for i in range(3):
-                        units[pl.ds(start + i, 1), :] = pieces_ref[
-                            x, y, z, c : c + 1, i * unit : (i + 1) * unit
+                        units[pl.ds(start + i, 1), :] = (own_ref, other_ref)[c][
+                            x, y, z, 0:1, i * unit : (i + 1) * unit
                         ]
     per_row = D // unit
     for row in range(12):
@@ -454,18 +456,18 @@
 COUNTS = (2, 2, 2, 4)
 
 
-def spread_vectors(owner, heads, pieces, unit, width):
+def spread_vectors(owner, heads, own, other, unit, width):
     outs = [like((12, D), F32), like((2, 8, FF // 2), F32), like((4, 8, width), F32)]
     return pl.pallas_call(
         spread_vectors_kernel,
-        in_specs=[SMEM_SPEC, SMEM_SPEC, pl.BlockSpec(memory_space=pltpu.VMEM)],
+        in_specs=[SMEM_SPEC, SMEM_SPEC] + [pl.BlockSpec(memory_space=pltpu.VMEM)] * 2,
         out_specs=[pl.BlockSpec(memory_space=pltpu.VMEM)] * 3,
         out_shape=outs,
         scratch_shapes=[pltpu.VMEM((12 * D // unit, unit), F32)],
         compiler_params=params(8),
         cost_estimate=cost(0.0, 0.5, 0.0),
         name="spread_vectors",
-    )(owner, heads, pieces)
+    )(owner, heads, own, other)
 
 
 def collect_vectors(owner, heads, unit, pair, *sources):
@@ -481,8 +483,8 @@
     )(owner, heads, *sources)
 
 
-def advance_attention_kernel(rates, *refs):
-    terms, olds, outs = refs[:2], refs[2:8], refs[8:]
+def advance_attention_kernel(rates, count, *refs):
+    terms, olds, outs = refs[:count], refs[count : count + 6], refs[count + 6 :]
     whole_sum = terms[0][...]
     for term in terms[1:]:
         whole_sum = whole_sum + term[...].astype(F32)
@@ -503,19 +505,21 @@
     outs[8][...] = whole_sum[rows : rows + 8]
 
 
-def advance_attention(terms, qkv, out, rates):
+def advance_attention(terms, qkv, out, rates, others):
     outs = [like(qkv[0].shape, F32)] * 4 + [like(out[0].shape, F32)] * 4
     outs.append(like((8, terms[0].shape[1]), F32))
     vmem = pl.BlockSpec(memory_space=pltpu.VMEM)
+    kernel = functools.partial(advance_attention_kernel, rates, len(terms))
+    kernel, corners, _ = waiting(kernel, others)
     return pl.pallas_call(
-        functools.partial(advance_attention_kernel, rates),
-        in_specs=[vmem] * 8,
+        kernel,
+        in_specs=[vmem] * (len(corners) + len(terms) + 6),
         out_specs=[vmem] * 9,
         out_shape=outs,
         compiler_params=params(16),
         cost_estimate=cost(0.0, 3.0, 0.0),
         name="advance_attention",
-    )(*terms, *qkv, *out)
+    )(*corners, *terms, *qkv, *out)
 
 
 def waiting(kernel, others):
@@ -530,18 +534,6 @@
 
 def per_part(array, size, by_x):
     return pl.BlockSpec((size, array.shape[1]), lambda g: (g // 2 if by_x else g % 2, 0))
-
-
-def attention_weights(weights, rows):
-    parts_qk, parts_vo = weights
-    specs = []
-    for part in parts_qk:
-        block = (1, part.shape[1], rows, part.shape[3])
-        specs.append(pl.BlockSpec(block, lambda g: (g, 0, 0, 0)))
-    for part in parts_vo:
-        block = (*part.shape[:2], rows, part.shape[3])
-        specs.append(pl.BlockSpec(block, lambda g: (0, 0, 0, 0)))
-    return [*parts_qk, *parts_vo], specs
 
 
 def params(mib):
@@ -558,7 +550,7 @@
 
 def attention_forward(place, x, weights, biases, half, mask, vec_rows, mix, rows):
     length = x.shape[0]
-    pair = weights[0][0].shape[3]
+    pair = weights[0].shape[4]
     width = pair // 2
     last = mix is not None
     row = like((length, D), F32)
@@ -569,9 +561,10 @@
     ]
     tail = [row]
     scratch = [pltpu.VMEM((D, pair), BF), pltpu.VMEM((D, pair), BF)]
-    operands, specs = attention_weights(weights, rows)
-    operands += [place, x, biases, mask, vec_rows]
-    specs += [
+    operands = [*weights, place, x, biases, mask, vec_rows]
+    specs = [
+        per_corner(weights[0], rows, 1),
+        per_corner(weights[1], rows, 0),
         SMEM_SPEC,
         whole(x),
         pl.BlockSpec((1, *biases.shape[1:]), lambda g: (half * 2 + g, 0, 0)),
@@ -585,7 +578,7 @@
         specs.append(whole(mix))
         scratch.append(pltpu.VMEM((length, D), F32))
     return pl.pallas_call(
-        functools.partial(attention_forward_kernel, rows, last, len(weights[0])),
+        functools.partial(attention_forward_kernel, rows, last),
         grid=(2,),
         in_specs=specs,
         out_specs=[per_group(o) for o in outs] + [whole(o) for o in tail],
@@ -599,10 +592,9 @@
 
 def attention_backward(place, x_t, gr, gr_t, weights, saved, mask, start, rows, last, others):
     length = gr.shape[0]
-    pair = weights[0][0].shape[3]
+    pair = weights[0].shape[4]
     width = pair // 2
-    across = len(weights[0])
-    deep = weights[0][0].shape[1]
+    across, _, deep = weights[0].shape[:3]
     qkv, lse, context = saved
     grad_qk = like((across, 2, deep, rows, pair), BF)
     grad_vo = like((2, across, deep, rows, pair), BF)
@@ -619,15 +611,15 @@
     ]
     if last:
         scratch.append(pltpu.VMEM((length, D), F32))
-    operands, specs = attention_weights(weights, rows)
-    kernel = functools.partial(attention_backward_kernel, rows, last, across)
+    kernel = functools.partial(attention_backward_kernel, rows, last)
     kernel, corners, corner_specs = waiting(kernel, others)
     return pl.pallas_call(
         kernel,
         grid=(2,),
         in_specs=corner_specs
-        + specs
         + [
+            per_corner(weights[0], rows, 1),
+            per_corner(weights[1], rows, 0),
             SMEM_SPEC,
             whole(x_t),
             whole(gr),
@@ -649,7 +641,7 @@
         compiler_params=params(18),
         cost_estimate=cost(0.5, 1.0, 0.1),
         name="attention_backward_last" if last else "attention_backward",
-    )(*corners, *operands, place, x_t, gr, gr_t, qkv, lse, context, mask, start)
+    )(*corners, *weights, place, x_t, gr, gr_t, qkv, lse, context, mask, start)
 
 
 def ffn_operands(up, down):
@@ -664,7 +656,7 @@
     hidden = 4 * chunk
     last = len(tail_operands) > 0
     row = like((length, D), F32)
-    outs = [like((length, hidden), BF), like((length, hidden), F32)]
+    outs = [like((length, hidden), BF), like((length, hidden), BF)]
     tail = [row]
     scratch = []
     if last:
@@ -776,20 +768,20 @@
     owner, group_head = owner.astype(jnp.int32), group_head.astype(jnp.int32)
 
     vec_row = jnp.pad(vectors.astype(BF), (0, pair - vec_len))[None]
-    vec_rows = jnp.pad(jnp.concatenate([vec_row, send(vec_row, "c")], 0), ((0, 6), (0, 0)))
+    vec_rows = jnp.pad(vec_row, ((0, 7), (0, 0)))
     pack_qk = jnp.concatenate([w_qkv[0], w_qkv[1]], 1).astype(BF)
     pack_vo = jnp.concatenate([w_qkv[2], w_out.T], 1).astype(BF)
     pack = jnp.concatenate([pack_qk, vec_rows, pack_vo], 0)
-    doc_x, x_y = to_documents(after(layer_input, vec_rows))
-    doc_cot, cot_y = to_documents(after(cotangent, vec_rows))
+    doc_x, x_y = to_documents(layer_input)
+    doc_cot, cot_y = to_documents(cotangent)
     attn_z, z_first = gather_z(pack)
     qk, vo = attn_z[:, : rows + 8], attn_z[:, rows + 8 :]
     qk_first, vo_first = send(qk, "y"), send(vo, "x")
-    qk = after(jnp.stack([qk, qk_first], 0), vo_first, x_y, cot_y)
+    qk = after(jnp.stack([qk, qk_first], 0), vo_first, x_y)
     vo = after(jnp.stack([vo, vo_first], 0), qk_first)
     qk_got, vo_got = send(qk, "x"), send(vo, "y")
-    attn_own = ((qk, qk_got), (vo, vo_got))
-    attn_other = jax.tree.map(lambda v: send(v, "c"), attn_own)
+    qk, vo = jnp.stack([qk, qk_got], 0), jnp.stack([vo, vo_got], 0)
+    qk_other, vo_other = send(qk, "c"), send(vo, "c")
 
     pack = jnp.concatenate([w_up.T.astype(BF), w_down.astype(BF)], 0)
     ffn_z, _ = gather_z(after(pack, z_first))
@@ -802,11 +794,14 @@
     )
     up_got, down_got = send(up, "x"), send(down, "y")
 
-    pieces = jnp.stack([qk[..., rows:, :], qk_got[..., rows:, :]], 0).astype(F32)
+    vec_own, vec_other = (v[..., rows:, :].astype(F32) for v in (qk, qk_other))
     if in_kernel:
-        vec_rows, bias_up, biases = spread_vectors(owner, group_head, pieces, ff_rows, head_cols)
+        vec_rows, bias_up, biases = spread_vectors(
+            owner, group_head, vec_own, vec_other, ff_rows, head_cols
+        )
     else:
-        vec_all = jnp.moveaxis(pieces[..., :2, :vec_len], -2, 0).reshape(blocks, vec_len)
+        vec_all = jnp.stack([v[..., 0, :vec_len] for v in (vec_own, vec_other)], 0)
+        vec_all = vec_all.reshape(blocks, vec_len)
         vec_rows = jnp.take(vec_all, seat, axis=0).reshape(12, D)
         bias_up = jnp.take(vec_rows[5:9].reshape(blocks, ff_rows), owner, axis=0)
         bias_up = jnp.pad(bias_up.reshape(2, 1, FF // 2), ((0, 0), (0, 7), (0, 0)))
@@ -831,12 +826,11 @@
         xs = x ^ jnp.arange(2)
         zs = flip_order("z")
 
-        def true_order(weights):
-            qk, vo = (jnp.stack(parts, 0)[..., :rows, :] for parts in weights)
-            qk = jnp.take(jnp.take(qk, xs, axis=0), zs, axis=2).transpose(1, 2, 0, 3, 4)
-            vo = jnp.take(jnp.take(vo, xs, axis=1), zs, axis=2).transpose(0, 2, 1, 3, 4)
-            qk, vo = qk.reshape(2, 1, D, pair), vo.reshape(2, 1, 1, D, pair)
-            return ((qk,), (vo[0], vo[1]))
+        def true_order(qk, vo):
+            qk = jnp.take(jnp.take(qk[..., :rows, :], xs, axis=0), zs, axis=2)
+            vo = jnp.take(jnp.take(vo, xs, axis=1), zs, axis=2)
+            qk, vo = qk.transpose(1, 2, 0, 3, 4), vo.transpose(0, 2, 1, 3, 4)
+            return qk.reshape(1, 2, 1, D, pair), vo.reshape(2, 1, 1, D, pair)
 
         def relative_order(qk, vo):
             qk = qk.reshape(2, deep, 2, rows, pair).transpose(2, 0, 1, 3, 4)
@@ -845,15 +839,16 @@
             return qk, jnp.take(jnp.take(vo, xs, axis=1), zs, axis=2)
 
         place = jnp.zeros((1,), jnp.int32)
-        attn_own, attn_other = true_order(attn_own), true_order(attn_other)
+        qk, vo = true_order(qk, vo)
+        qk_other, vo_other = true_order(qk_other, vo_other)
         kernel_rows = D
     place = place.astype(jnp.int32)
 
     *saved_0, mix = attention_forward(
-        place, doc_x, attn_own, biases, 0, mask_row, vec_rows, None, kernel_rows
+        place, doc_x, (qk, vo), biases, 0, mask_row, vec_rows, None, kernel_rows
     )
     *saved_1, hidden, hidden_b, normed, inverse, x_t = attention_forward(
-        place, doc_x, attn_other, biases, 1, mask_row, vec_rows, mix, kernel_rows
+        place, doc_x, (qk_other, vo_other), biases, 1, mask_row, vec_rows, mix, kernel_rows
     )
     flat = lambda v: v.reshape(FF // 4, D)
     up_own, down_own = (flat(up), flat(up_got)), (flat(down), flat(down_got))
@@ -881,7 +876,7 @@
         down_own,
         d_hidden,
         (normed, inverse, vec_rows),
-        (out_y,),
+        (),
     )
     grad_up = swap([up_0.reshape(lead), up_1.reshape(lead)], "x")
     grad_down = swap([down_0.reshape(lead), down_1.reshape(lead)], "y")
@@ -889,13 +884,13 @@
     ffn_big = (grad_up[-1], grad_down[-1])
     grad_up, grad_down = swap(grad_up, "y"), swap(grad_down, "x")
     ffn_second = (grad_up[-1], grad_down[-1])
-    grad_ffn = scatter_z([grad_up, grad_down])
+    grad_ffn, _ = scatter_z([grad_up, grad_down], False)
 
     qk_1, vo_1, bias_1, d_attn = attention_backward(
-        place, x_t, d_first_b, d_first_t, attn_other, saved_1, mask_col, d_first, kernel_rows, False, ffn_c
+        place, x_t, d_first_b, d_first_t, (qk_other, vo_other), saved_1, mask_col, d_first, kernel_rows, False, (ffn_c, out_y)
     )
     qk_0, vo_0, bias_0, d_input = attention_backward(
-        place, x_t, d_first_b, d_first_t, attn_own, saved_0, mask_col, d_attn, kernel_rows, True, ()
+        place, x_t, d_first_b, d_first_t, (qk, vo), saved_0, mask_col, d_attn, kernel_rows, True, ()
     )
     if not in_kernel:
         qk_1, vo_1 = relative_order(qk_1, vo_1)
@@ -940,9 +935,9 @@
         vec_terms = [t[0] for t in vec_terms] + [got[..., rows:, :]]
         sum_vo = swap(sum_vo, axis_vo, ffn_second)
     d_input = after(d_input, got, sum_vo[-1])
-    grad_ffn = after(total(grad_ffn), got, sum_vo[-1])
+    grad_attn, sent = scatter_z([sum_qk, vec_terms, sum_vo], True)
+    grad_ffn = after(total(grad_ffn), sent)
     grad_up, grad_down = grad_ffn[:ff_rows].T, grad_ffn[ff_rows:]
-    grad_attn = scatter_z([sum_qk, vec_terms, sum_vo])
     layer_output = from_documents(group_head, after(out_own, grad_ffn), out_y, BF)
     grad_input = from_documents(group_head, *from_documents_y(d_input, local), F32)
 
@@ -961,7 +956,9 @@
             new_mom_out,
             new_avg_out,
             grad_vec,
-        ) = advance_attention(grad_attn, olds_qkv, olds_out, (rate, rate_out))
+        ) = advance_attention(
+            grad_attn, olds_qkv, olds_out, (rate, rate_out), (layer_output, grad_input)
+        )
         grad_vec = grad_vec[0, :vec_len]
     else:
         grad_attn = total(grad_attn)

time: 276 us -> 234 us (0.85)
  waiting for transfers between devices: 95.6 us -> 73.7 us
  other arithmetic: 26.1 us -> 11.7 us
  local copies, waits for them, and re-layouts: 24.7 us -> 17.9 us
  starting transfers between devices: 38.7 us -> 42.5 us
    ppermute x46 -> x44, waiting for transfers between devices: 95.6 us -> 73.7 us  [send(): lax.ppermute(values, axis, [(i, i ^ bit) for i in range(lax.axis_size(axi...]
    unnamed x95 -> x53, local copies, waits for them, and re-layouts: 13 us -> 2.54 us
    another operation x11 -> x10, other arithmetic: 8.76 us -> 2.23 us
    ppermute x46 -> x44, starting transfers between devices: 38.7 us -> 42.5 us  [send(): lax.ppermute(values, axis, [(i, i ^ bit) for i in range(lax.axis_size(axi...]
    slice x18 -> x17, local copies, waits for them, and re-layouts: 9.3 us -> 8.74 us  [after(): corner(v)[0, 0].astype(F32) * 0.0]
  transfers between devices with their start and end apart: 46 -> 44, of which waited for: 20 -> 21; matrix products, arithmetic and copies ran while one was open for 13% -> 10% of each run, Pallas kernels for 20% -> 23%
where the time goes in v1:
time: 234 us; the launch traced here: 230 us
  waiting for transfers between devices  73.7 us (31%)
  Pallas kernels  70.5 us (30%)
  starting transfers between devices  42.5 us (18%)
  local copies, waits for them, and re-layouts  17.9 us (8%)
  between operations  13.5 us (6%)
  other arithmetic  11.7 us (5%)
    ppermute x44, waiting for transfers between devices, send(): lax.ppermute(values, axis, [(i, i ^ bit) for i in range(lax.axis_size(axi...  73.7 us
    ppermute x44, starting transfers between devices, send(): lax.ppermute(values, axis, [(i, i ^ bit) for i in range(lax.axis_size(axi...  42.5 us
    pallas_call x2, Pallas kernels, attention_backward(): pl.pallas_call(kernel, grid=(2,), in_specs=corner_specs + [per_corner(wei...  22 us
    pallas_call x2, Pallas kernels, ffn_backward(): pl.pallas_call(kernel, grid=(4,), in_specs=corner_specs + specs + [whole(...  16.5 us
    pallas_call x2, Pallas kernels, ffn_forward(): pl.pallas_call(functools.partial(ffn_forward_kernel, last), grid=(4,), in...  14 us
    pallas_call x2, Pallas kernels, attention_forward(): pl.pallas_call(functools.partial(attention_forward_kernel, rows, last), g...  13.4 us
    slice x17, local copies, waits for them, and re-layouts, after(): corner(v)[0, 0].astype(F32) * 0.0  8.74 us
  transfers between devices with their start and end apart: 44, of which 21 were waited for; matrix products, arithmetic and copies ran while one was open for 10% of the time, Pallas kernels for 23%

profile of v1, /device:TPU:0, one launch (start us, length us, event | category | flops | bytes accessed | tf_op | source)
XLA Modules:
  0.0 229.7 jit_solution(12519219640146110028)
XLA Ops:
  4.2 4.0 %collective-permute-start = (bf16[200,384]{1,0:T(8,128)(2,1)}, bf16[200,384]{1,0:T(8,128)(2,1)S(1)}, u32[]{:S(2)}, u32[]{:S(2)}) collective-permute-start(bf16[200,384]{1,0:T(8,128)(2,1)} %fusion.17), channel_id=1, source_target_pairs={{0,16},{8,24},{16,0},{24,8},{1,17},{9,25},{17,1},{25,9},{2,18},{10... | collective-permute-start | bytes 460808 | tf_op jit(solution)/shard_map/ppermute | solution.py:30
  14.1 1.6 collective-permute-done
  17.9 3.3 %collective-permute-start.1 = (bf16[192,768]{1,0:T(8,128)(2,1)S(1)}, bf16[192,768]{1,0:T(8,128)(2,1)S(1)}, u32[]{:S(2)}, u32[]{:S(2)}) collective-permute-start(bf16[192,768]{1,0:T(8,128)(2,1)S(1)} %maximum_add_fusion.10), channel_id=1, source_target_pairs={{0,16},{8,24},{16,0},{24,8},{1,17},{9,25},{17,1},{25,9},{2,18},{10... | collective-permute-start | bytes 884744 | tf_op jit(solution)/shard_map/ppermute | solution.py:30
  22.1 6.3 %collective-permute-done.20 = bf16[2,128,768]{2,1,0:T(8,128)(2,1)} collective-permute-done((bf16[2,128,768]{2,1,0:T(8,128)(2,1)}, bf16[2,128,768]{2,1,0:T(8,128)(2,1)}, u32[]{:S(2)}, u32[]{:S(2)}) %collective-permute-start.20) | collective-permute-done | bytes 393248 | tf_op jit(solution)/shard_map/ppermute | solution.py:30
  31.6 2.9 %collective-permute-done.1 = bf16[192,768]{1,0:T(8,128)(2,1)S(1)} collective-permute-done((bf16[192,768]{1,0:T(8,128)(2,1)S(1)}, bf16[192,768]{1,0:T(8,128)(2,1)S(1)}, u32[]{:S(2)}, u32[]{:S(2)}) %collective-permute-start.1) | collective-permute-done | bytes 294944 | tf_op jit(solution)/shard_map/ppermute | solution.py:30
  38.1 4.7 %collective-permute-done.5 = bf16[4,96,384]{2,1,0:T(8,128)(2,1)S(1)} collective-permute-done((bf16[4,96,384]{2,1,0:T(8,128)(2,1)S(1)}, bf16[4,96,384]{2,1,0:T(8,128)(2,1)S(1)}, u32[]{:S(2)}, u32[]{:S(2)}) %collective-permute-start.5) | collective-permute-done | bytes 294944 | tf_op jit(solution)/shard_map/ppermute | solution.py:30
  47.0 1.6 collective-permute-start.10
  49.2 1.6 collective-permute-start.6
  52.3 11.2 %collective-permute-done.9 = bf16[2,4,104,384]{3,2,1,0:T(8,128)(2,1)S(1)} collective-permute-done((bf16[2,4,104,384]{3,2,1,0:T(8,128)(2,1)S(1)}, bf16[2,4,104,384]{3,2,1,0:T(8,128)(2,1)S(1)}, u32[]{:S(2)}, u32[]{:S(2)}) %collective-permute-start.9) | collective-permute-done | bytes 639008 | tf_op jit(solution)/shard_map/ppermute | solution.py:30
  66.8 6.1 %collective-permute-done.6 = bf16[4,96,768]{2,1,0:T(8,128)(2,1)S(1)} collective-permute-done((bf16[4,96,768]{2,1,0:T(8,128)(2,1)S(1)}, bf16[4,96,768]{2,1,0:T(8,128)(2,1)S(1)}, u32[]{:S(2)}, u32[]{:S(2)}) %collective-permute-start.6) | collective-permute-done | bytes 589856 | tf_op jit(solution)/shard_map/ppermute | solution.py:30
  74.2 1.6 collective-permute-start.18
  79.1 6.3 %attention_forward.1 = (bf16[2,512,576]{2,1,0:T(8,128)(2,1)S(1)}, f32[2,8,512]{2,1,0:T(8,128)S(1)}, bf16[2,512,192]{2,1,0:T(8,128)(2,1)S(1)}, f32[512,768]{1,0:T(8,128)S(1)}) custom-call(bf16[2,2,4,104,384]{4,3,2,1,0:T(8,128)(2,1)S(1)} %pad_maximum_fusion.refs_0_, bf16[2,2,4,96,384]{4,3,2,1,0:T(8,128)(2,1)S(1)} %pad_maximum_fusion.2.refs_1_, ...), custom_call_target="tpu_custom_call" | custom-call | flops 4499999744 | bytes 6000000 | tf_op jit(solution)/shard_map/attention_forward/pallas_call | solution.py:580
  86.1 7.1 %attention_forward_last.1 = (bf16[2,512,576]{2,1,0:T(8,128)(2,1)S(1)}, f32[2,8,512]{2,1,0:T(8,128)S(1)}, bf16[2,512,192]{2,1,0:T(8,128)(2,1)S(1)}, f32[512,768]{...) custom-call(bf16[2,2,4,104,384]{4,3,2,1,0:T(8,128)(2,1)S(1)} %collec, ...), custom_call_target="tpu_custom_call" | custom-call | flops 4499999744 | bytes 6000000 | tf_op jit(solution)/shard_map/attention_forward_last/pallas_call | solution.py:580
  94.3 4.8 %collective-permute-done.18 = bf16[2,4,96,768]{3,2,1,0:T(8,128)(2,1)S(1)} collective-permute-done((bf16[2,4,96,768]{3,2,1,0:T(8,128)(2,1)S(1)}, bf16[2,4,96,768]{3,2,1,0:T(8,128)(2,1)S(1)}, u32[]{:S(2)}, u32[]{:S(2)}) %collective-permute-start.18) | collective-permute-done | bytes 1179680 | tf_op jit(solution)/shard_map/ppermute | solution.py:30
  99.4 2.4 %collective-permute-done.12 = bf16[2,4,96,768]{3,2,1,0:T(8,128)(2,1)S(1)} collective-permute-done((bf16[2,4,96,768]{3,2,1,0:T(8,128)(2,1)S(1)}, bf16[2,4,96,768]{3,2,1,0:T(8,128)(2,1)S(1)}, u32[]{:S(2)}, u32[]{:S(2)}) %collective-permute-start.12) | collective-permute-done | bytes 1179680 | tf_op jit(solution)/shard_map/ppermute | solution.py:30
  102.1 6.2 %ffn_forward.1 = (bf16[512,1536]{1,0:T(8,128)(2,1)S(1)}, bf16[512,1536]{1,0:T(8,128)(2,1)S(1)}, f32[512,768]{1,0:T(8,128)S(1)}) custom-call(bf16[768,768]{1,0:T(8,128)(2,1)S(1)} %bitcast.456, bf16[768,768]{1,0:T(8,128)(2,1)S(1)} %bitcast.458, bf16[768,768]{1,0:T(8,128)(2,1)S(1)} %bitcast.451, bf16[768,768]{1,0:T(8,128)(2,1)S(1)} %bitcast.453, ...), custom_call_target="tpu_custom_call" | custom-call | flops 4899999744 | bytes 12000000 | tf_op jit(solution)/shard_map/ffn_forward/pallas_call | solution.py:666
  108.5 7.7 %ffn_forward_last.1 = (bf16[512,1536]{1,0:T(8,128)(2,1)S(1)}, bf16[512,1536]{1,0:T(8,128)(2,1)S(1)}, bf16[512,768]{1,0:T(8,128)(2,1)S(1)}, f32[512,768]{1,0:T(8,...) custom-call(bf16[768,768]{1,0:T(8,128)(2,1)S(1)} %collective-permute-done.11.refs_0_, ...), custom_call_target="tpu_custom_call" | custom-call | flops 4899999744 | bytes 12000000 | tf_op jit(solution)/shard_map/ffn_forward_last/pallas_call | solution.py:666
  116.3 7.8 %ffn_backward.1 = (bf16[1536,768]{1,0:T(8,128)(2,1)S(1)}, bf16[1536,768]{1,0:T(8,128)(2,1)S(1)}, f32[8,1536]{1,0:T(8,128)S(1)}, f32[512,768]{1,0:T(8,128)S(1)}) custom-call(bf16[768,768]{1,0:T(8,128)(2,1)S(1)} %collective-permute-done.11.refs_0_, bf16[768,768]{1,0:T(8,128)(2,1)S(1)} %collective-permute-done.16.refs_1_, ...), custom_call_target="tpu_custom_call" | custom-call | flops 9699999744 | bytes 16000000 | tf_op jit(solution)/shard_map/ffn_backward/pallas_call | solution.py:695
  125.3 8.7 %ffn_backward_last.1 = (bf16[1536,768]{1,0:T(8,128)(2,1)S(1)}, bf16[1536,768]{1,0:T(8,128)(2,1)S(1)}, f32[8,1536]{1,0:T(8,128)S(1)}, f32[512,768]{1,0:T(8,128)S(...) custom-call(bf16[768,768]{1,0:T(8,128)(2,1)S(1)} %bitcast.457, ...), custom_call_target="tpu_custom_call" | custom-call | flops 9699999744 | bytes 16000000 | tf_op jit(solution)/shard_map/ffn_backward_last/pallas_call | solution.py:695
  134.0 2.2 collective-permute-done.30.got_y_ref
  138.6 10.9 %attention_backward.1 = (bf16[2,2,4,96,384]{4,3,2,1,0:T(8,128)(2,1)S(1)}, bf16[2,2,4,96,384]{4,3,2,1,0:T(8,128)(2,1)S(1)}, f32[2,8,192]{2,1,0:T(8,128)S(1)}, f32[512,768]{1,0:T(8,128)S(1)}) custom-call(bf16[8,128]{1,0:T(8,128)(2,1)S(1)} %slice_bitcast_fusion.68.refs_0_, bf16[8,128]{1,0:T(8,128)(2,1)S(1)} %slice_bitcast_fusion.67.refs_1_, ...), custom_call_target="tpu_custom_call" | custom-call | flops 500000000 | bytes 1000000 | tf_op jit(solution)/shard_map/attention_backward/pallas_call | solution.py:616
  150.1 11.2 %attention_backward_last.1 = (bf16[2,2,4,96,384]{4,3,2,1,0:T(8,128)(2,1)S(1)}, bf16[2,2,4,96,384]{4,3,2,1,0:T(8,128)(2,1)S(1)}, f32[2,8,192]{2,1,0:T(8,128)S(1)}, bf16[512,768]{1,0:T(8,128)(2,1)S(1)}) custom-call(bf16[2,2,4,104,384]{4,3,2,1,0:T(8,128)(2,1)S(1)} %pad_maximum_fusion.refs_0_, bf16[2,2,4,96,384]{4,3,2,1,0:T(8,128)(2,1)S(1)} %pad_maximum_fusion.2.refs_1_, ...), custom_call_target="tpu_custom_call" | custom-call | flops 500000000 | bytes 1000000 | tf_op jit(solution)/shard_map/attention_backward_last/pallas_call | solution.py:616
  161.7 2.9 %collective-permute-done.23 = bf16[2,4,96,768]{3,2,1,0:T(8,128)(2,1)S(1)} collective-permute-done((bf16[2,4,96,768]{3,2,1,0:T(8,128)(2,1)S(1)}, bf16[2,4,96,768]{3,2,1,0:T(8,128)(2,1)S(1)}, u32[]{:S(2)}, u32[]{:S(2)}) %collective-permute-start.23) | collective-permute-done | bytes 1179680 | tf_op jit(solution)/shard_map/ppermute | solution.py:30
  171.6 7.1 %collective-permute-done.24 = bf16[4,96,768]{2,1,0:T(8,128)(2,1)S(1)} collective-permute-done((bf16[4,96,768]{2,1,0:T(8,128)(2,1)S(1)}, bf16[4,96,768]{2,1,0:T(8,128)(2,1)S(1)}, u32[]{:S(2)}, u32[]{:S(2)}) %collective-permute-start.24) | collective-permute-done | bytes 589856 | tf_op jit(solution)/shard_map/ppermute | solution.py:30
  185.2 9.3 %collective-permute-done.37 = bf16[2,4,96,384]{3,2,1,0:T(8,128)(2,1)S(1)} collective-permute-done((bf16[2,4,96,384]{3,2,1,0:T(8,128)(2,1)S(1)}, bf16[2,4,96,384]{3,2,1,0:T(8,128)(2,1)S(1)}, u32[]{:S(2)}, u32[]{:S(2)}) %collective-permute-start.37) | collective-permute-done | bytes 589856 | tf_op jit(solution)/shard_map/ppermute | solution.py:30
  196.0 2.6 %collective-permute-start.29 = (bf16[192,768]{1,0:T(8,128)(2,1)S(1)}, bf16[192,768]{1,0:T(8,128)(2,1)S(1)}, u32[]{:S(2)}, u32[]{:S(2)}) collective-permute-start(bf16[192,768]{1,0:T(8,128)(2,1)S(1)} %pad_maximum_fusion.15), channel_id=1, source_target_pairs={{0,16},{8,24},{16,0},{24,8},{1,17},{9,25},{17,1},{25,9},{2,18},{10... | collective-permute-start | bytes 884744 | tf_op jit(solution)/shard_map/ppermute | solution.py:30
  198.7 2.2 collective-permute-done.33
  202.0 2.0 collective-permute-done.38
  204.7 3.4 %collective-permute-done.34 = bf16[4,104,384]{2,1,0:T(8,128)(2,1)S(1)} collective-permute-done((bf16[4,104,384]{2,1,0:T(8,128)(2,1)S(1)}, bf16[4,104,384]{2,1,0:T(8,128)(2,1)S(1)}, u32[]{:S(2)}, u32[]{:S(2)}) %collective-permute-start.34) | collective-permute-done | bytes 319520 | tf_op jit(solution)/shard_map/ppermute | solution.py:30
  208.3 2.4 %collective-permute-start.43 = (bf16[200,384]{1,0:T(8,128)(2,1)S(1)}, bf16[200,384]{1,0:T(8,128)(2,1)S(1)}, u32[]{:S(2)}, u32[]{:S(2)}) collective-permute-start(bf16[200,384]{1,0:T(8,128)(2,1)S(1)} %pad_maximum_fusion.18), channel_id=1, source_target_pairs={{0,24},{8,16},{16,8},{24,0},{1,25},{9,17},{17,9},{25,1},{2,26},{10... | collective-permute-start | bytes 460808 | tf_op jit(solution)/shard_map/ppermute | solution.py:30
  210.9 2.1 collective-permute-start.41
  220.8 1.9 collective-permute-done.39.got_y_ref
  (272 shorter events, 60.0 us)
Async XLA Ops:
  9.1 12.4 %collective-permute-start.8 = (bf16[2,128,768]{2,1,0:T(8,128)(2,1)}, bf16[2,128,768]{2,1,0:T(8,128)(2,1)}, u32[]{:S(2)}, u32[]{:S(2)}) collective-permute-start(bf16[2,128,768]{2,1,0:T(8,128)(2,1)} %dynamic-slice_bitcast_fusion.1), channel_id=1, source_target_pairs={{0,2},{2,0},{1,3},{3,1},{4,6},{6,4},{5,7},{7,5},{8,10},{10,8},{9,1... | collective-permute-start | bytes 1179656 | tf_op jit(solution)/shard_map/ppermute | solution.py:30
  11.5 16.9 %collective-permute-start.20 = (bf16[2,128,768]{2,1,0:T(8,128)(2,1)}, bf16[2,128,768]{2,1,0:T(8,128)(2,1)}, u32[]{:S(2)}, u32[]{:S(2)}) collective-permute-start(bf16[2,128,768]{2,1,0:T(8,128)(2,1)} %dynamic-slice_bitcast_fusion), channel_id=1, source_target_pairs={{0,2},{2,0},{1,3},{3,1},{4,6},{6,4},{5,7},{7,5},{8,10},{10,8},{9,1... | collective-permute-start | bytes 1179656 | tf_op jit(solution)/shard_map/ppermute | solution.py:30
  15.8 18.9 %collective-permute-start.3 = (bf16[2,200,384]{2,1,0:T(8,128)(2,1)S(1)}, bf16[2,200,384]{2,1,0:T(8,128)(2,1)S(1)}, u32[]{:S(2)}, u32[]{:S(2)}) collective-permute-start(bf16[2,200,384]{2,1,0:T(8,128)(2,1)S(1)} %pad_maximum_fusion.12), channel_id=1, source_target_pairs={{0,8},{8,0},{16,24},{24,16},{1,9},{9,1},{17,25},{25,17},{2,10},{10... | collective-permute-start | bytes 921608 | tf_op jit(solution)/shard_map/ppermute | solution.py:30
  17.9 16.6 %collective-permute-start.1 = (bf16[192,768]{1,0:T(8,128)(2,1)S(1)}, bf16[192,768]{1,0:T(8,128)(2,1)S(1)}, u32[]{:S(2)}, u32[]{:S(2)}) collective-permute-start(bf16[192,768]{1,0:T(8,128)(2,1)S(1)} %maximum_add_fusion.10), channel_id=1, source_target_pairs={{0,16},{8,24},{16,0},{24,8},{1,17},{9,25},{17,1},{25,9},{2,18},{10... | collective-permute-start | bytes 884744 | tf_op jit(solution)/shard_map/ppermute | solution.py:30
  30.9 17.8 %collective-permute-start.15 = (bf16[2,128,768]{2,1,0:T(8,128)(2,1)S(1)}, bf16[2,128,768]{2,1,0:T(8,128)(2,1)S(1)}, u32[]{:S(2)}, u32[]{:S(2)}) collective-permute-start(bf16[2,128,768]{2,1,0:T(8,128)(2,1)S(1)} %pad_maximum_fusion.8), channel_id=1, source_target_pairs={{0,1},{1,0},{2,3},{3,2},{4,5},{5,4},{6,7},{7,6},{8,9},{9,8},{10,11... | collective-permute-start | bytes 1179656 | tf_op jit(solution)/shard_map/ppermute | solution.py:30
  31.0 71.0 %collective-permute-start.21 = (bf16[2,128,768]{2,1,0:T(8,128)(2,1)S(1)}, bf16[2,128,768]{2,1,0:T(8,128)(2,1)S(1)}, u32[]{:S(2)}, u32[]{:S(2)}) collective-permute-start(bf16[2,128,768]{2,1,0:T(8,128)(2,1)S(1)} %pad_maximum_fusion.9), channel_id=1, source_target_pairs={{0,1},{1,0},{2,3},{3,2},{4,5},{5,4},{6,7},{7,6},{8,9},{9,8},{10,11... | collective-permute-start | bytes 1179656 | tf_op jit(solution)/shard_map/ppermute | solution.py:30
  34.6 14.5 %collective-permute-start.2 = (bf16[2,192,768]{2,1,0:T(8,128)(2,1)S(1)}, bf16[2,192,768]{2,1,0:T(8,128)(2,1)S(1)}, u32[]{:S(2)}, u32[]{:S(2)}) collective-permute-start(bf16[2,192,768]{2,1,0:T(8,128)(2,1)S(1)} %pad_maximum_fusion.6), channel_id=1, source_target_pairs={{0,8},{8,0},{16,24},{24,16},{1,9},{9,1},{17,25},{25,17},{2,10},{10... | collective-permute-start | bytes 1769480 | tf_op jit(solution)/shard_map/ppermute | solution.py:30
  46.1 17.4 %collective-permute-start.9 = (bf16[2,4,104,384]{3,2,1,0:T(8,128)(2,1)S(1)}, bf16[2,4,104,384]{3,2,1,0:T(8,128)(2,1)S(1)}, u32[]{:S(2)}, u32[]{:S(2)}) collective-permute-start(bf16[2,4,104,384]{3,2,1,0:T(8,128)(2,1)S(1)} %maximum_add_fusion.3), channel_id=1, source_target_pairs={{0,4},{4,0},{1,5},{5,1},{2,6},{6,2},{3,7},{7,3},{8,12},{12,8},{9,1... | collective-permute-start | bytes 1916936 | tf_op jit(solution)/shard_map/ppermute | solution.py:30
  47.0 16.7 %collective-permute-start.10 = (bf16[2,4,96,384]{3,2,1,0:T(8,128)(2,1)S(1)}, bf16[2,4,96,384]{3,2,1,0:T(8,128)(2,1)S(1)}, u32[]{:S(2)}, u32[]{:S(2)}) collective-permute-start(bf16[2,4,96,384]{3,2,1,0:T(8,128)(2,1)S(1)} %maximum_add_fusion.6), channel_id=1, source_target_pairs={{0,2},{2,0},{1,3},{3,1},{4,6},{6,4},{5,7},{7,5},{8,10},{10,8},{9,1... | collective-permute-start | bytes 1769480 | tf_op jit(solution)/shard_map/ppermute | solution.py:30
  49.2 23.6 %collective-permute-start.6 = (bf16[4,96,768]{2,1,0:T(8,128)(2,1)S(1)}, bf16[4,96,768]{2,1,0:T(8,128)(2,1)S(1)}, u32[]{:S(2)}, u32[]{:S(2)}) collective-permute-start(bf16[4,96,768]{2,1,0:T(8,128)(2,1)S(1)} %get-tuple-element.150), channel_id=1, source_target_pairs={{0,2},{2,0},{1,3},{3,1},{4,6},{6,4},{5,7},{7,5},{8,10},{10,8},{9,1... | collective-permute-start | bytes 1769480 | tf_op jit(solution)/shard_map/ppermute | solution.py:30
  50.8 23.2 %collective-permute-start.7 = (bf16[4,96,768]{2,1,0:T(8,128)(2,1)S(1)}, bf16[4,96,768]{2,1,0:T(8,128)(2,1)S(1)}, u32[]{:S(2)}, u32[]{:S(2)}) collective-permute-start(bf16[4,96,768]{2,1,0:T(8,128)(2,1)S(1)} %get-tuple-element.149), channel_id=1, source_target_pairs={{0,4},{4,0},{1,5},{5,1},{2,6},{6,2},{3,7},{7,3},{8,12},{12,8},{9,1... | collective-permute-start | bytes 1769480 | tf_op jit(solution)/shard_map/ppermute | solution.py:30
  63.6 14.5 %collective-permute-start.13 = (bf16[2,2,4,104,384]{4,3,2,1,0:T(8,128)(2,1)S(1)}, bf16[2,2,4,104,384]{4,3,2,1,0:T(8,128)(2,1)S(1)}, u32[]{:S(2)}, u32[]{:S(2)}) collective-permute-start(bf16[2,2,4,104,384]{4,3,2,1,0:T(8,128)(2,1)S(1)} %pad_maximum_fusion.refs_0_), channel_id=1, source_target_pairs={{0,1},{1,0},{2,3},{3,2},{4,5},{5,4},{6,7},{7,6},{8,9},{9,8},{10,11... | collective-permute-start | bytes 3833864 | tf_op jit(solution)/shard_map/ppermute | solution.py:30
  65.0 20.4 %collective-permute-start.14 = (bf16[2,2,4,96,384]{4,3,2,1,0:T(8,128)(2,1)S(1)}, bf16[2,2,4,96,384]{4,3,2,1,0:T(8,128)(2,1)S(1)}, u32[]{:S(2)}, u32[]{:S(2)}) collective-permute-start(bf16[2,2,4,96,384]{4,3,2,1,0:T(8,128)(2,1)S(1)} %pad_maximum_fusion.2.refs_1_), channel_id=1, source_target_pairs={{0,1},{1,0},{2,3},{3,2},{4,5},{5,4},{6,7},{7,6},{8,9},{9,8},{10,11... | collective-permute-start | bytes 3538952 | tf_op jit(solution)/shard_map/ppermute | solution.py:30
  74.2 25.0 %collective-permute-start.18 = (bf16[2,4,96,768]{3,2,1,0:T(8,128)(2,1)S(1)}, bf16[2,4,96,768]{3,2,1,0:T(8,128)(2,1)S(1)}, u32[]{:S(2)}, u32[]{:S(2)}) collective-permute-start(bf16[2,4,96,768]{3,2,1,0:T(8,128)(2,1)S(1)} %maximum_add_fusion.2), channel_id=1, source_target_pairs={{0,2},{2,0},{1,3},{3,1},{4,6},{6,4},{5,7},{7,5},{8,10},{10,8},{9,1... | collective-permute-start | bytes 3538952 | tf_op jit(solution)/shard_map/ppermute | solution.py:30
  77.1 24.7 %collective-permute-start.12 = (bf16[2,4,96,768]{3,2,1,0:T(8,128)(2,1)S(1)}, bf16[2,4,96,768]{3,2,1,0:T(8,128)(2,1)S(1)}, u32[]{:S(2)}, u32[]{:S(2)}) collective-permute-start(bf16[2,4,96,768]{3,2,1,0:T(8,128)(2,1)S(1)} %maximum_add_fusion.1), channel_id=1, source_target_pairs={{0,4},{4,0},{1,5},{5,1},{2,6},{6,2},{3,7},{7,3},{8,12},{12,8},{9,1... | collective-permute-start | bytes 3538952 | tf_op jit(solution)/shard_map/ppermute | solution.py:30
  78.2 30.2 %collective-permute-start.17 = (bf16[768,768]{1,0:T(8,128)(2,1)S(1)}, bf16[768,768]{1,0:T(8,128)(2,1)S(1)}, u32[]{:S(2)}, u32[]{:S(2)}) collective-permute-start(bf16[768,768]{1,0:T(8,128)(2,1)S(1)} %bitcast.450), channel_id=1, source_target_pairs={{0,1},{1,0},{2,3},{3,2},{4,5},{5,4},{6,7},{7,6},{8,9},{9,8},{10,11... | collective-permute-start | bytes 3538952 | tf_op jit(solution)/shard_map/ppermute | solution.py:30
  85.5 22.9 %collective-permute-start.11 = (bf16[768,768]{1,0:T(8,128)(2,1)S(1)}, bf16[768,768]{1,0:T(8,128)(2,1)S(1)}, u32[]{:S(2)}, u32[]{:S(2)}) collective-permute-start(bf16[768,768]{1,0:T(8,128)(2,1)S(1)} %bitcast.455), channel_id=1, source_target_pairs={{0,1},{1,0},{2,3},{3,2},{4,5},{5,4},{6,7},{7,6},{8,9},{9,8},{10,11... | collective-permute-start | bytes 3538952 | tf_op jit(solution)/shard_map/ppermute | solution.py:30
  124.1 12.2 %collective-permute-start.22 = (bf16[1536,768]{1,0:T(8,128)(2,1)S(1)}, bf16[1536,768]{1,0:T(8,128)(2,1)S(1)}, u32[]{:S(2)}, u32[]{:S(2)}) collective-permute-start(bf16[1536,768]{1,0:T(8,128)(2,1)S(1)} %get-tuple-element.92), channel_id=1, source_target_pairs={{0,1},{1,0},{2,3},{3,2},{4,5},{5,4},{6,7},{7,6},{8,9},{9,8},{10,11... | collective-permute-start | bytes 7077896 | tf_op jit(solution)/shard_map/ppermute | solution.py:30
  124.6 13.1 %collective-permute-start.25 = (bf16[1536,768]{1,0:T(8,128)(2,1)S(1)}, bf16[1536,768]{1,0:T(8,128)(2,1)S(1)}, u32[]{:S(2)}, u32[]{:S(2)}) collective-permute-start(bf16[1536,768]{1,0:T(8,128)(2,1)S(1)} %get-tuple-element.94), channel_id=1, source_target_pairs={{0,1},{1,0},{2,3},{3,2},{4,5},{5,4},{6,7},{7,6},{8,9},{9,8},{10,11... | collective-permute-start | bytes 7077896 | tf_op jit(solution)/shard_map/ppermute | solution.py:30
  137.0 27.5 %collective-permute-start.23 = (bf16[2,4,96,768]{3,2,1,0:T(8,128)(2,1)S(1)}, bf16[2,4,96,768]{3,2,1,0:T(8,128)(2,1)S(1)}, u32[]{:S(2)}, u32[]{:S(2)}) collective-permute-start(bf16[2,4,96,768]{3,2,1,0:T(8,128)(2,1)S(1)} %bitcast.497), channel_id=1, source_target_pairs={{0,4},{4,0},{1,5},{5,1},{2,6},{6,2},{3,7},{7,3},{8,12},{12,8},{9,1... | collective-permute-start | bytes 3538952 | tf_op jit(solution)/shard_map/ppermute | solution.py:30
  138.1 27.3 %collective-permute-start.26 = (bf16[2,4,96,768]{3,2,1,0:T(8,128)(2,1)S(1)}, bf16[2,4,96,768]{3,2,1,0:T(8,128)(2,1)S(1)}, u32[]{:S(2)}, u32[]{:S(2)}) collective-permute-start(bf16[2,4,96,768]{3,2,1,0:T(8,128)(2,1)S(1)} %bitcast.496), channel_id=1, source_target_pairs={{0,2},{2,0},{1,3},{3,1},{4,6},{6,4},{5,7},{7,5},{8,10},{10,8},{9,1... | collective-permute-start | bytes 3538952 | tf_op jit(solution)/shard_map/ppermute | solution.py:30
  149.5 20.7 %collective-permute-start.31 = (bf16[2,2,4,96,384]{4,3,2,1,0:T(8,128)(2,1)S(1)}, bf16[2,2,4,96,384]{4,3,2,1,0:T(8,128)(2,1)S(1)}, u32[]{:S(2)}, u32[]{:S(2)}) collective-permute-start(bf16[2,2,4,96,384]{4,3,2,1,0:T(8,128)(2,1)S(1)} %get-tuple-element.107), channel_id=1, source_target_pairs={{0,1},{1,0},{2,3},{3,2},{4,5},{5,4},{6,7},{7,6},{8,9},{9,8},{10,11... | collective-permute-start | bytes 3538952 | tf_op jit(solution)/shard_map/ppermute | solution.py:30
  149.6 31.5 %collective-permute-start.36 = (bf16[2,2,4,96,384]{4,3,2,1,0:T(8,128)(2,1)S(1)}, bf16[2,2,4,96,384]{4,3,2,1,0:T(8,128)(2,1)S(1)}, u32[]{:S(2)}, u32[]{:S(2)}) collective-permute-start(bf16[2,2,4,96,384]{4,3,2,1,0:T(8,128)(2,1)S(1)} %get-tuple-element.116), channel_id=1, source_target_pairs={{0,1},{1,0},{2,3},{3,2},{4,5},{5,4},{6,7},{7,6},{8,9},{9,8},{10,11... | collective-permute-start | bytes 3538952 | tf_op jit(solution)/shard_map/ppermute | solution.py:30
  164.7 14.1 %collective-permute-start.24 = (bf16[4,96,768]{2,1,0:T(8,128)(2,1)S(1)}, bf16[4,96,768]{2,1,0:T(8,128)(2,1)S(1)}, u32[]{:S(2)}, u32[]{:S(2)}) collective-permute-start(bf16[4,96,768]{2,1,0:T(8,128)(2,1)S(1)} %fusion.2), channel_id=1, source_target_pairs={{0,2},{2,0},{1,3},{3,1},{4,6},{6,4},{5,7},{7,5},{8,10},{10,8},{9,1... | collective-permute-start | bytes 1769480 | tf_op jit(solution)/shard_map/ppermute | solution.py:30
  165.5 13.8 %collective-permute-start.27 = (bf16[4,96,768]{2,1,0:T(8,128)(2,1)S(1)}, bf16[4,96,768]{2,1,0:T(8,128)(2,1)S(1)}, u32[]{:S(2)}, u32[]{:S(2)}) collective-permute-start(bf16[4,96,768]{2,1,0:T(8,128)(2,1)S(1)} %fusion.1), channel_id=1, source_target_pairs={{0,4},{4,0},{1,5},{5,1},{2,6},{6,2},{3,7},{7,3},{8,12},{12,8},{9,1... | collective-permute-start | bytes 1769480 | tf_op jit(solution)/shard_map/ppermute | solution.py:30
  181.3 13.1 %collective-permute-start.37 = (bf16[2,4,96,384]{3,2,1,0:T(8,128)(2,1)S(1)}, bf16[2,4,96,384]{3,2,1,0:T(8,128)(2,1)S(1)}, u32[]{:S(2)}, u32[]{:S(2)}) collective-permute-start(bf16[2,4,96,384]{3,2,1,0:T(8,128)(2,1)S(1)} %fusion.4), channel_id=1, source_target_pairs={{0,2},{2,0},{1,3},{3,1},{4,6},{6,4},{5,7},{7,5},{8,10},{10,8},{9,1... | collective-permute-start | bytes 1769480 | tf_op jit(solution)/shard_map/ppermute | solution.py:30
  183.0 12.6 %collective-permute-start.28 = (bf16[2,192,768]{2,1,0:T(8,128)(2,1)S(1)}, bf16[2,192,768]{2,1,0:T(8,128)(2,1)S(1)}, u32[]{:S(2)}, u32[]{:S(2)}) collective-permute-start(bf16[2,192,768]{2,1,0:T(8,128)(2,1)S(1)} %pad_maximum_fusion.7), channel_id=1, source_target_pairs={{0,8},{8,0},{16,24},{24,16},{1,9},{9,1},{17,25},{25,17},{2,10},{10... | collective-permute-start | bytes 1769480 | tf_op jit(solution)/shard_map/ppermute | solution.py:30
  184.4 16.5 %collective-permute-start.33 = (bf16[2,4,104,384]{3,2,1,0:T(8,128)(2,1)S(1)}, bf16[2,4,104,384]{3,2,1,0:T(8,128)(2,1)S(1)}, u32[]{:S(2)}, u32[]{:S(2)}) collective-permute-start(bf16[2,4,104,384]{3,2,1,0:T(8,128)(2,1)S(1)} %fusion), channel_id=1, source_target_pairs={{0,4},{4,0},{1,5},{5,1},{2,6},{6,2},{3,7},{7,3},{8,12},{12,8},{9,1... | collective-permute-start | bytes 1916936 | tf_op jit(solution)/shard_map/ppermute | solution.py:30
  196.0 21.0 %collective-permute-start.29 = (bf16[192,768]{1,0:T(8,128)(2,1)S(1)}, bf16[192,768]{1,0:T(8,128)(2,1)S(1)}, u32[]{:S(2)}, u32[]{:S(2)}) collective-permute-start(bf16[192,768]{1,0:T(8,128)(2,1)S(1)} %pad_maximum_fusion.15), channel_id=1, source_target_pairs={{0,16},{8,24},{16,0},{24,8},{1,17},{9,25},{17,1},{25,9},{2,18},{10... | collective-permute-start | bytes 884744 | tf_op jit(solution)/shard_map/ppermute | solution.py:30
  208.3 18.7 %collective-permute-start.43 = (bf16[200,384]{1,0:T(8,128)(2,1)S(1)}, bf16[200,384]{1,0:T(8,128)(2,1)S(1)}, u32[]{:S(2)}, u32[]{:S(2)}) collective-permute-start(bf16[200,384]{1,0:T(8,128)(2,1)S(1)} %pad_maximum_fusion.18), channel_id=1, source_target_pairs={{0,24},{8,16},{16,8},{24,0},{1,25},{9,17},{17,9},{25,1},{2,26},{10... | collective-permute-start | bytes 460808 | tf_op jit(solution)/shard_map/ppermute | solution.py:30
  210.8 16.2 %collective-permute-start.42 = (bf16[200,384]{1,0:T(8,128)(2,1)S(1)}, bf16[200,384]{1,0:T(8,128)(2,1)S(1)}, u32[]{:S(2)}, u32[]{:S(2)}) collective-permute-start(bf16[200,384]{1,0:T(8,128)(2,1)S(1)} %pad_maximum_fusion.17), channel_id=1, source_target_pairs={{0,8},{8,0},{16,24},{24,16},{1,9},{9,1},{17,25},{25,17},{2,10},{10... | collective-permute-start | bytes 460808 | tf_op jit(solution)/shard_map/ppermute | solution.py:30
  210.9 16.1 %collective-permute-start.41 = (bf16[200,384]{1,0:T(8,128)(2,1)S(1)}, bf16[200,384]{1,0:T(8,128)(2,1)S(1)}, u32[]{:S(2)}, u32[]{:S(2)}) collective-permute-start(bf16[200,384]{1,0:T(8,128)(2,1)S(1)} %pad_maximum_fusion.16), channel_id=1, source_target_pairs={{0,16},{8,24},{16,0},{24,8},{1,17},{9,25},{17,1},{25,9},{2,18},{10... | collective-permute-start | bytes 460808 | tf_op jit(solution)/shard_map/ppermute | solution.py:30
  (39 other events, 142.7 us)
